TPU v7x, 512 devices: a whole 4x8x8 slice. The times are simulated.
512 devices in a mesh: ctx: 32 (over y, z_hi), head: 16 (over z_lo, x, core).
Axes of the slice: x: 4, y: 8, z: 8 (z_hi: 4, z_lo: 2; z = z_hi * 2 + z_lo), core: 2. Of those that a mesh axis runs over, the one named last changes fastest.
Arguments:
- block_owner: int32 [64], P('ctx'), may hold values from 0 to 63, each once
- query_nope: bfloat16 [4096, 8192], P('ctx', 'head'), may hold values from -6 to 6
- query_rope: bfloat16 [4096, 4096], P('ctx', 'head'), may hold values from -90 to 90
- latent_cache: bfloat16 [4096, 576], P('ctx'), may hold values from -6 to 6, as said below
- key_up_weight: bfloat16 [512, 8192], P(None, 'head'), may hold values from -0.25 to 0.25
- value_up_weight: bfloat16 [512, 8192], P(None, 'head'), may hold values from -0.25 to 0.25
- saved_output: bfloat16 [4096, 32768], P('ctx', 'head'), may hold values from -4 to 4
- output_grad: bfloat16 [4096, 8192], P('ctx', 'head'), may hold values from -6 to 6
Outputs:
- grad_query_nope: bfloat16 [4096, 8192], P('ctx', 'head')
- grad_query_rope: bfloat16 [4096, 4096], P('ctx', 'head')
- grad_latent: bfloat16 [4096, 512], P('ctx')
- grad_key_up: float32 [512, 8192], P(None, 'head')
- grad_value_up: float32 [512, 8192], P(None, 'head')
Inputs may be any that keep to these rules, and one draw needn't show every extreme that they name: `latent_cache`: in every row the first 512 entries are the latent and the last 64 the rotary key.
All inputs are finite; a program needn't handle non-finite values.
Results may differ from a plain program's by a relative error of at most 0.03.
Values may be sent and summed in bfloat16 or wider, within the bound.
A program may use at most 64 MiB of HBM per device.

v0:
```python
import math

import jax
import jax.numpy as jnp
from jax import lax
from jax.sharding import PartitionSpec as P

LATENT = 512
ROPE = 64
NOPE = 128


def sweep_blocks(block_step, carried, key_rows, key_positions, start_row):
    key_count = key_rows.shape[0]
    block_size = math.gcd(key_count, 512)
    block_turns = key_count // block_size

    def block_turn(block_index, running):
        offset_rows = block_index * block_size
        return block_step(
            running,
            lax.dynamic_slice_in_dim(key_rows, offset_rows, block_size, 0),
            lax.dynamic_slice_in_dim(key_positions, offset_rows, block_size, 0),
            start_row + offset_rows,
        )

    return lax.fori_loop(0, block_turns, block_turn, carried)


def on_device(
    block_owner,
    query_nope,
    query_rope,
    latent_cache,
    key_up_weight,
    value_up_weight,
    saved_output,
    output_grad,
):
    row_count = query_nope.shape[0]
    head_count = query_rope.shape[1] // ROPE
    half_rows = row_count // 2
    group_rows = head_count * row_count
    softmax_scale = (NOPE + ROPE) ** (-0.5)
    local_positions = (
        block_owner[:, None] * half_rows + jnp.arange(half_rows, dtype=jnp.int32)[None, :]
    ).reshape(row_count)
    query_split = query_nope.reshape(row_count, head_count, NOPE)
    key_weight = key_up_weight.reshape(LATENT, head_count, NOPE)
    value_weight = value_up_weight.reshape(LATENT, head_count, NOPE)
    output_split = output_grad.reshape(row_count, head_count, NOPE)
    saved_split = saved_output.reshape(row_count, head_count, LATENT)
    absorbed = (
        jnp.einsum("thd,lhd->htl", query_split, key_weight, preferred_element_type=jnp.float32)
        .astype(jnp.bfloat16)
        .reshape(group_rows, LATENT)
    )
    rotary_rows = (
        query_rope.reshape(row_count, head_count, ROPE).transpose(1, 0, 2).reshape(group_rows, ROPE)
    )
    queries = jnp.concatenate([absorbed, rotary_rows], 1)
    query_positions = jnp.tile(local_positions, head_count)
    latest_query = jnp.max(local_positions)
    latent_grad_out = (
        jnp.einsum("thd,lhd->htl", output_split, value_weight, preferred_element_type=jnp.float32)
        .astype(jnp.bfloat16)
        .reshape(group_rows, LATENT)
    )
    saved_rows = saved_split.transpose(1, 0, 2).reshape(group_rows, LATENT)
    row_delta = jnp.sum(latent_grad_out.astype(jnp.float32) * saved_rows.astype(jnp.float32), 1)

    def masked_scores(key_rows, key_positions):
        raw_scores = (
            jnp.einsum("rf,kf->rk", queries, key_rows, preferred_element_type=jnp.float32)
            * softmax_scale
        )
        visible = key_positions[None, :] <= query_positions[:, None]
        return (jnp.where(visible, raw_scores, -1e30), visible)

    def stat_step(carried, key_rows, key_positions, start_row):

        def stat_compute_block(running):
            running_max, running_sum = running
            masked, visible = masked_scores(key_rows, key_positions)
            new_max = jnp.maximum(running_max, jnp.max(masked, 1))
            weights = jnp.where(visible, jnp.exp(masked - new_max[:, None]), 0.0)
            return (new_max, running_sum * jnp.exp(running_max - new_max) + jnp.sum(weights, 1))

        def skip_block(running):
            return running

        return lax.cond(
            jnp.min(key_positions) <= latest_query, stat_compute_block, skip_block, carried
        )

    stat_start = (
        jnp.full((group_rows,), -1e30, jnp.float32),
        jnp.zeros((group_rows,), jnp.float32),
    )
    all_keys, all_positions = (
        lax.all_gather(latent_cache, "ctx", axis=0, tiled=True),
        lax.all_gather(local_positions, "ctx", axis=0, tiled=True),
    )
    running_max, running_sum = sweep_blocks(stat_step, stat_start, all_keys, all_positions, 0)
    log_norm = running_max + jnp.log(running_sum)

    def block_terms(key_rows, key_positions):
        masked, visible = masked_scores(key_rows, key_positions)
        probabilities = jnp.where(visible, jnp.exp(masked - log_norm[:, None]), 0.0)
        probs_low = probabilities.astype(jnp.bfloat16)
        prob_grad = jnp.einsum(
            "rl,kl->rk", latent_grad_out, key_rows[:, :LATENT], preferred_element_type=jnp.float32
        )
        score_grad = (probabilities * (prob_grad - row_delta[:, None]) * softmax_scale).astype(
            jnp.bfloat16
        )
        return (probs_low, score_grad)

    def key_side(score_grad, probs_low):
        return jnp.einsum(
            "rk,rl->kl", score_grad, absorbed, preferred_element_type=jnp.float32
        ) + jnp.einsum("rk,rl->kl", probs_low, latent_grad_out, preferred_element_type=jnp.float32)

    total_rows = row_count * lax.axis_size("ctx")
    query_start = jnp.zeros((group_rows, LATENT + ROPE), jnp.float32)

    def grad_step(carried, key_rows, key_positions, start_row):
        query_grad, latent_buffer = carried

        def grad_compute_block(running):
            probs_low, score_grad = block_terms(key_rows, key_positions)
            running = running + jnp.dot(score_grad, key_rows, preferred_element_type=jnp.float32)
            return (running, key_side(score_grad, probs_low))

        def empty_block(running):
            return (running, jnp.zeros((key_rows.shape[0], LATENT), jnp.float32))

        query_grad, key_block = lax.cond(
            jnp.min(key_positions) <= latest_query, grad_compute_block, empty_block, query_grad
        )
        latent_buffer = lax.dynamic_update_slice_in_dim(latent_buffer, key_block, start_row, 0)
        return (query_grad, latent_buffer)

    grad_start = (query_start, jnp.zeros((total_rows, LATENT), jnp.float32))
    grad_result = sweep_blocks(grad_step, grad_start, all_keys, all_positions, 0)
    query_grad = grad_result[0]
    absorbed_grad = (
        query_grad[:, :LATENT].astype(jnp.bfloat16).reshape(head_count, row_count, LATENT)
    )
    grad_query_rope = (
        query_grad[:, LATENT:]
        .astype(jnp.bfloat16)
        .reshape(head_count, row_count, ROPE)
        .transpose(1, 0, 2)
        .reshape(row_count, head_count * ROPE)
    )
    grad_query_nope = (
        jnp.einsum("htl,lhd->thd", absorbed_grad, key_weight, preferred_element_type=jnp.float32)
        .astype(jnp.bfloat16)
        .reshape(row_count, head_count * NOPE)
    )
    key_part = jnp.einsum(
        "htl,thd->lhd", absorbed_grad, query_split, preferred_element_type=jnp.float32
    ).reshape(LATENT, head_count * NOPE)
    value_part = jnp.einsum(
        "thl,thd->lhd", saved_split, output_split, preferred_element_type=jnp.float32
    ).reshape(LATENT, head_count * NOPE)
    grad_key_up, grad_value_up = (
        lax.psum(key_part.astype(jnp.bfloat16), "ctx").astype(jnp.float32),
        lax.psum(value_part.astype(jnp.bfloat16), "ctx").astype(jnp.float32),
    )
    latent_shares = lax.psum_scatter(
        grad_result[1].astype(jnp.bfloat16), "ctx", scatter_dimension=0, tiled=True
    )
    grad_latent = lax.psum(latent_shares, "head")
    return (grad_query_nope, grad_query_rope, grad_latent, grad_key_up, grad_value_up)


def solution(mesh):
    return jax.shard_map(
        on_device,
        mesh=mesh,
        in_specs=(
            P("ctx"),
            P("ctx", "head"),
            P("ctx", "head"),
            P("ctx", None),
            P(None, "head"),
            P(None, "head"),
            P("ctx", "head"),
            P("ctx", "head"),
        ),
        out_specs=(
            P("ctx", "head"),
            P("ctx", "head"),
            P("ctx", None),
            P(None, "head"),
            P(None, "head"),
        ),
        check_vma=False,
    )
```

profile of v0, /device:TPU:1, one launch (start us, length us, event | category | flops | bytes accessed | tf_op | source)
XLA Modules:
  0.0 927.6 jit_solution(3368628551974083834)
XLA Ops:
  17.4 73.7 %all-gather = s32[32,1,128]{2,1,0:T(1,128)S(1)} all-gather(s32[1,1,128]{2,1,0:T(1,128)S(1)} %reshape.94), channel_id=1, replica_groups=mesh['ctx'=32,'head'=16] {'ctx'}, dimensions={0}, use_global_device_ids=true | all-gather | bytes 16896 | tf_op jit(solution)/shard_map/all_gather | solution.py:102
  92.5 35.9 %all-gather.3.cloned.1.call-done = bf16[4096,576]{1,0:T(8,128)(2,1)} async-done(((bf16[128,576]{1,0:T(8,128)(2,1)}), bf16[4096,576]{1,0:T(8,128)(2,1)}) %all-gather.3.cloned.1.call-update) | async-done | bytes 4718608 | tf_op jit(solution)/shard_map/all_gather | solution.py:101
  128.4 38.0 %while.35 = (s32[]{:T(128)}, f32[512]{0:T(512)S(1)}, f32[512]{0:T(512)S(1)}, s32[4096]{0:T(1024)S(1)}, s32[]{:T(128)}, /*index=5*/bf16[4096,576]{1,0:T(8,128)(2,...) while((s32[]{:T(128)}, f32[512]{0:T(512)S(1)}, ...), condition=%wide.region_7.8_spmd.clone, body=%wide.region_1.7_spmd.clone.sunk | while | flops 304088576 | bytes 3384601 | solution.py:27
  130.5 2.6 conditional.6
  135.3 2.6 conditional.6
  140.0 2.6 conditional.6
  144.8 2.6 conditional.6
  149.6 2.6 conditional.6
  154.3 2.6 conditional.6
  159.1 2.6 conditional.6
  163.8 2.6 conditional.6
  167.5 2.3 broadcast_in_dim.37
  169.8 71.9 %while.36 = (s32[]{:T(128)}, f32[512,576]{0,1:T(8,128)S(1)}, bf16[4096,512]{1,0:T(8,128)(2,1)}, s32[4096]{0:T(1024)S(1)}, s32[]{:T(128)}, /*index=5*/bf16[4096,5...) while((s32[]{:T(128)}, f32[512,576]{0,1:T(8,128)S(1)}, ...), condition=%wide.region_13.14_spmd.clone, body=%wide.region_9.13_spmd.clone.sunk | while | flops 1412727296 | bytes 14828345 | solution.py:27
  171.7 6.1 conditional.7
  171.8 2.0 fusion.16
  180.7 6.1 conditional.7
  189.7 6.1 conditional.7
  189.7 2.0 fusion.16
  198.7 6.1 conditional.7
  207.6 6.1 conditional.7
  207.7 2.0 fusion.16
  216.6 6.1 conditional.7
  216.6 2.0 fusion.16
  225.6 6.1 conditional.7
  225.6 2.0 fusion.16
  234.6 6.1 conditional.7
  234.6 2.0 fusion.16
  245.8 222.9 %reduce-scatter.2.cloned.1.call-done = bf16[128,512]{1,0:T(8,128)(2,1)} async-done(((bf16[4096,512]{1,0:T(8,128)(2,1)}), bf16[128,512]{1,0:T(8,128)(2,1)}) %reduce-scatter.2.cloned.1.call-update) | async-done | bytes 131088 | tf_op jit(solution)/shard_map/reduce_scatter | solution.py:172
  470.6 303.9 %all-reduce.6.cloned.1.call-done = (bf16[512,512]{1,0:T(8,128)(2,1)}, bf16[512,512]{1,0:T(8,128)(2,1)}) async-done(((bf16[512,512]{1,0:T(8,128)(2,1)}, bf16[512,512]{1,0:T(8,128)(2,1)}), (bf16[512,512]{1,0:T(8,128)(2,1)}, bf16[512,512]{1,0:T(8,128)(2,1)})) %all-reduce.6.cloned.1.call-update) | async-done | bytes 1048592 | tf_op jit(solution)/shard_map/psum | solution.py:169
  774.5 2.1 convert_element_type.85
  776.7 2.1 convert_element_type.89
  778.8 140.7 %all-reduce.4.cloned.1.call-done = bf16[128,512]{1,0:T(8,128)(2,1)} async-done(((bf16[128,512]{1,0:T(8,128)(2,1)}), bf16[128,512]{1,0:T(8,128)(2,1)}) %all-reduce.4.cloned.1.call-update) | async-done | bytes 131088 | tf_op jit(solution)/shard_map/psum | solution.py:175
  (175 shorter events, 96.3 us)
Async XLA Ops:
  7.2 84.3 %copy-start = (bf16[512,512]{1,0:T(8,128)(2,1)S(1)}, bf16[512,512]{1,0:T(8,128)(2,1)}, u32[]{:S(2)}) copy-start(bf16[512,512]{1,0:T(8,128)(2,1)} %param.21) | copy-start | bytes 1572868
  7.2 121.3 %all-gather.3.cloned.1.call-start = ((), (), s32[]{:S(2)}) async-start(), calls=%async_computation.1 | async-start | bytes 5406720 | tf_op jit(solution)/shard_map/all_gather | solution.py:101
  9.0 459.7 %reduce-scatter.2.cloned.1.call-start = ((), (), s32[]{:S(2)}) async-start(), calls=%async_computation.2 | async-start | bytes 4325376 | tf_op jit(solution)/shard_map/reduce_scatter | solution.py:172
  14.3 114.1 %copy-start.5 = (bf16[128,512]{0,1:T(8,128)(2,1)}, bf16[128,512]{0,1:T(8,128)(2,1)S(1)}, u32[]{:S(2)}) copy-start(bf16[128,512]{0,1:T(8,128)(2,1)S(1)} %copy.93) | copy-start | bytes 393220
  15.6 75.9 %copy-start.1 = (bf16[512,512]{0,1:T(8,128)(2,1)}, bf16[512,512]{0,1:T(8,128)(2,1)S(1)}, u32[]{:S(2)}) copy-start(bf16[512,512]{0,1:T(8,128)(2,1)S(1)} %copy.92) | copy-start | bytes 1572868
  17.1 73.9 %copy-start.3 = (bf16[128,2048]{0,1:T(8,128)(2,1)}, bf16[128,2048]{0,1:T(8,128)(2,1)S(1)}, u32[]{:S(2)}) copy-start(bf16[128,2048]{0,1:T(8,128)(2,1)S(1)} %copy.76) | copy-start | bytes 1572868
  166.5 0.8 copy-start.7
  166.5 3.3 copy-start.8
  166.5 3.3 copy-start.9
  241.6 1.0 copy-start.4
  241.6 1.1 copy-start.6
  241.7 532.9 %all-reduce.6.cloned.1.call-start = ((), (), s32[]{:S(2)}) async-start(), calls=%async_computation.4 | async-start | bytes 2097152 | tf_op jit(solution)/shard_map/psum | solution.py:169
  243.0 225.7 %copy-start.2 = (bf16[512,512]{0,1:T(8,128)(2,1)S(1)}, bf16[512,512]{0,1:T(8,128)(2,1)}, u32[]{:S(2)}) copy-start(bf16[512,512]{0,1:T(8,128)(2,1)} %copy-done.1) | copy-start | bytes 1572868
  245.7 673.8 %all-reduce.4.cloned.1.call-start = ((), (), s32[]{:S(2)}) async-start(), calls=%async_computation.3 | async-start | bytes 262144 | tf_op jit(solution)/shard_map/psum | solution.py:175
Sparse Core Ops, SparseCore 0:
  11.8 116.6 all-gather.2
  241.8 226.8 reduce-scatter.1
  472.5 301.9 all-reduce.5
  777.3 142.2 all-reduce.3
where the time goes:
time: 930 us; the launch traced here: 928 us
  waiting for transfers between devices  704 us (76%)
  blocking collectives  73.7 us (8%)
  matrix products  64.6 us (7%)
  local copies, waits for them, and re-layouts  30.2 us (3%)
  loops' own time  21.4 us (2%)
  other arithmetic  19.9 us (2%)
  between operations  14 us (2%)
    psum x1, waiting for transfers between devices, on_device(): lax.psum(key_part.astype(jnp.bfloat16), 'ctx').astype(jnp.float32)  304 us
    reduce_scatter x1, waiting for transfers between devices, on_device(): lax.psum_scatter(grad_result[1].astype(jnp.bfloat16), 'ctx', scatter_dime...  223 us
    psum x1, waiting for transfers between devices, on_device(): grad_latent = lax.psum(latent_shares, 'head')  141 us
    all_gather x1, blocking collectives, on_device(): lax.all_gather(local_positions, 'ctx', axis=0, tiled=True)  73.7 us
    all_gather x1, waiting for transfers between devices, on_device(): lax.all_gather(latent_cache, 'ctx', axis=0, tiled=True)  35.9 us
    dot_general x16, matrix products, masked_scores(): jnp.einsum('rf,kf->rk', queries, key_rows, preferred_element_type=jnp.flo...  29.8 us
    another operation x2, loops' own time, sweep_blocks(): return lax.fori_loop(0, block_turns, block_turn, carried)  20.8 us
  transfers between devices with their start and end apart: 4, of which 4 were waited for; matrix products, arithmetic and copies ran while one was open for 2% of the time, Pallas kernels for 0%

commit v1 on v0

v1 whole, which is shorter than its diff:
```python
import functools
import math

import jax
import jax.numpy as jnp
from jax import lax
from jax.experimental import pallas as pl
from jax.experimental.pallas import tpu as pltpu
from jax.sharding import PartitionSpec as P

LATENT = 512
ROPE = 64
NOPE = 128
NY, NZH, NX = 8, 4, 4
NZ = 2 * NZH
BLOCKS = 64
WIDE = LATENT + ROPE + BLOCKS
TOK = 128
CHUNK = 512
HIDDEN = -1e30
BF16 = jnp.bfloat16
F32 = jnp.float32
VMEM_LIMIT = 58 * 1024 * 1024


def place():
    ctx, head = lax.axis_index("ctx"), lax.axis_index("head")
    y, zh = ctx // NZH, lax.rem(ctx, NZH)
    zl = head // (2 * NX)
    x = lax.rem(head // 2, NX)
    core = lax.rem(head, 2)
    return y, zh, zl, x, core


def device(y, zh, zl, x, core):
    return (y * NZH + zh, zl * (2 * NX) + x * 2 + core)


def copy_to(src, dst, send_sem, recv_sem, target):
    return pltpu.make_async_remote_copy(
        src_ref=src,
        dst_ref=dst,
        send_sem=send_sem,
        recv_sem=recv_sem,
        device_id=target,
        device_id_type=pl.DeviceIdType.MESH,
    )


def greet(peers):
    barrier = pltpu.get_barrier_semaphore()
    for peer in peers:
        pl.semaphore_signal(barrier, inc=1, device_id=peer, device_id_type=pl.DeviceIdType.MESH)
    pl.semaphore_wait(barrier, len(peers))


def wrap(index, size):
    return lax.rem(index + 2 * size, size)


def gather_kernel(
    owner, latent, keys, near_send, near_recv, y_send, y_recv, z_send, z_recv, core_send, core_recv
):
    y, zh, zl, x, core = place()
    turn = 1 - 2 * core
    z = 2 * zh + zl
    sibling = device(y, zh, zl, x, 1 - core)
    y_peers = [device(wrap(y + d, NY), zh, zl, x, core) for d in range(1, NY)]
    zh_peers = [device(y, wrap(zh + d, NZH), zl, x, core) for d in range(1, NZH)]

    def z_device(where):
        return device(y, where // 2, lax.rem(where, 2), x, core)

    ring_peers = [z_device(wrap(z + 1, NZ)), z_device(wrap(z - 1, NZ))]

    column = lax.broadcasted_iota(jnp.int32, (16, BLOCKS), 1)
    for half in range(2):
        mark = jnp.where(column == owner[half], 1.0, 0.0).astype(BF16)
        for part in range(2):
            for low in range(2):
                start = half * 64 + part * 32 + low * 16
                keys[y, zh, half, part, low, :, : LATENT + ROPE] = latent[pl.ds(start, 16), :]
                keys[y, zh, half, part, low, :, LATENT + ROPE :] = mark

    greet([sibling] + y_peers + zh_peers + ring_peers)

    first = []
    for d in range(1, NZH):
        region = keys.at[y, zh, core, 0]
        first.append(copy_to(region, region, near_send.at[d - 1], near_recv.at[d - 1], zh_peers[d - 1]))
    for d in range(1, NY):
        region = keys.at[y, zh, core, 1, zl]
        slot = NZH - 1 + d - 1
        first.append(copy_to(region, region, near_send.at[slot], near_recv.at[slot], y_peers[d - 1]))
    for copy in first:
        copy.start()

    passed = []

    def pass_on(region):
        slot = len(passed)
        copy = copy_to(region, region, core_send.at[slot], core_recv.at[slot], sibling)
        copy.start()
        other = 1 - core
        passed.append(copy)

    half_y, half_z = NZH // 2, NY // 2
    y_next = device(wrap(y + turn, NY), zh, zl, x, core)
    z_next = z_device(wrap(z + turn, NZ))

    def y_copy(step, sub):
        where = wrap(y - turn * step, NY)
        region = keys.at[where, pl.ds(sub * half_y, half_y), core, 0]
        return copy_to(region, region, y_send.at[step, sub], y_recv.at[step, sub], y_next)

    def y_arrived(step, sub):
        where = wrap(y - turn * (step + 1), NY)
        region = keys.at[where, pl.ds(sub * half_y, half_y), core, 0]
        return copy_to(region, region, y_send.at[step, sub], y_recv.at[step, sub], y_next)

    def z_region(where, sub):
        return keys.at[pl.ds(sub * half_z, half_z), where // 2, core, 1, lax.rem(where, 2)]

    def z_copy(step, sub):
        region = z_region(wrap(z - turn * step, NZ), sub)
        return copy_to(region, region, z_send.at[step, sub], z_recv.at[step, sub], z_next)

    def z_arrived(step, sub):
        region = z_region(wrap(z - turn * (step + 1), NZ), sub)
        return copy_to(region, region, z_send.at[step, sub], z_recv.at[step, sub], z_next)

    for d in range(1, NZH):
        region = keys.at[y, wrap(zh - d, NZH), core, 0]
        copy_to(region, region, near_send.at[d - 1], near_recv.at[d - 1], zh_peers[d - 1]).wait_recv()
    for sub in range(2):
        y_copy(0, sub).start()
    for d in range(1, NY):
        region = keys.at[wrap(y - d, NY), zh, core, 1, zl]
        slot = NZH - 1 + d - 1
        copy_to(region, region, near_send.at[slot], near_recv.at[slot], y_peers[d - 1]).wait_recv()
    for sub in range(2):
        z_copy(0, sub).start()
    for d in range(1, NZH):
        pass_on(keys.at[y, wrap(zh - d, NZH), core, 0])
    pass_on(keys.at[:, zh, core, 1, zl])
    for copy in first:
        copy.wait_send()

    for step in range(max(NY, NZ) - 1):
        for sub in range(2):
            if step < NY - 1:
                y_arrived(step, sub).wait_recv()
                if step + 1 < NY - 1:
                    y_copy(step + 1, sub).start()
            if step < NZ - 1:
                z_arrived(step, sub).wait_recv()
                if step + 1 < NZ - 1:
                    z_copy(step + 1, sub).start()
        if step < NY - 1:
            pass_on(keys.at[wrap(y - turn * (step + 1), NY), :, core, 0])
        if step < NZ - 1:
            where = wrap(z - turn * (step + 1), NZ)
            pass_on(keys.at[:, where // 2, core, 1, lax.rem(where, 2)])
    for step in range(NY - 1):
        for sub in range(2):
            y_copy(step, sub).wait_send()
    for step in range(NZ - 1):
        for sub in range(2):
            z_copy(step, sub).wait_send()
    for copy in passed:
        copy.wait_send()
    slot = 0
    other = 1 - core
    arrivals = [keys.at[y, wrap(zh - d, NZH), other, 0] for d in range(1, NZH)]
    arrivals.append(keys.at[:, zh, other, 1, zl])
    for step in range(max(NY, NZ) - 1):
        if step < NY - 1:
            arrivals.append(keys.at[wrap(y + turn * (step + 1), NY), :, other, 0])
        if step < NZ - 1:
            where = wrap(z + turn * (step + 1), NZ)
            arrivals.append(keys.at[:, where // 2, other, 1, lax.rem(where, 2)])
    for slot, region in enumerate(arrivals):
        copy_to(region, region, core_send.at[slot], core_recv.at[slot], sibling).wait_recv()


def gather_keys(owner, latent):
    passes = NZH - 1 + 1 + (NY - 1) + (NZ - 1)
    near = NZH - 1 + NY - 1
    dma = pltpu.SemaphoreType.DMA
    return pl.pallas_call(
        gather_kernel,
        out_shape=jax.ShapeDtypeStruct((NY, NZH, 2, 2, 2, 16, WIDE), BF16),
        in_specs=[
            pl.BlockSpec(memory_space=pltpu.SMEM),
            pl.BlockSpec(memory_space=pltpu.VMEM),
        ],
        out_specs=pl.BlockSpec(memory_space=pltpu.VMEM),
        scratch_shapes=[
            dma((near,)),
            dma((near,)),
            dma((NY - 1, 2)),
            dma((NY - 1, 2)),
            dma((NZ - 1, 2)),
            dma((NZ - 1, 2)),
            dma((passes,)),
            dma((passes,)),
        ],
        compiler_params=pltpu.CompilerParams(
            collective_id=0, has_side_effects=True, vmem_limit_bytes=VMEM_LIMIT
        ),
        name="gather_keys",
    )(owner, latent)


def dot(left, right):
    return jnp.dot(left, right, preferred_element_type=F32)


def dot_nt(left, right):
    return lax.dot_general(left, right, (((1,), (1,)), ((), ())), preferred_element_type=F32)


def dot_tn(left, right):
    return lax.dot_general(left, right, (((0,), (0,)), ((), ())), preferred_element_type=F32)


def attention_kernel(
    owner,
    keys,
    query_nope,
    query_rope,
    key_weight,
    value_weight,
    saved,
    output_grad,
    grad_nope,
    grad_rope,
    latent_part,
    weight_part,
    query_t,
    absorbed,
    grad_out_t,
    grad_out,
    delta,
    weights,
    prob_grad,
    tops,
    sums,
    query_grad,
):
    heads = query_nope.shape[1] // NOPE
    rows = heads * TOK
    scale = (NOPE + ROPE) ** -0.5
    log2_scale = scale * math.log2(math.e)
    chunks = keys.shape[0] // CHUNK
    own = lax.axis_index("ctx")

    rope_t = query_rope[...].astype(F32).T.astype(BF16)
    block = lax.broadcasted_iota(jnp.int32, (BLOCKS, TOK), 0)
    token = lax.broadcasted_iota(jnp.int32, (BLOCKS, TOK), 1)
    limit = jnp.where(token < TOK // 2, owner[0], owner[1])
    bias = jnp.where(block <= limit, 0.0, HIDDEN).astype(BF16)
    for h in range(heads):
        cols = slice(h * NOPE, (h + 1) * NOPE)
        span = slice(h * TOK, (h + 1) * TOK)
        query, weight = query_nope[:, cols], key_weight[:, cols]
        absorbed[span, :] = dot_nt(query, weight).astype(BF16)
        query_t[:LATENT, span] = dot_nt(weight, query).astype(BF16)
        query_t[LATENT : LATENT + ROPE, span] = rope_t[h * ROPE : (h + 1) * ROPE, :]
        query_t[LATENT + ROPE :, span] = bias
        out, weight = output_grad[:, cols], value_weight[:, cols]
        grads = dot_nt(out, weight).astype(BF16)
        grad_out[span, :] = grads
        grad_out_t[:, span] = dot_nt(weight, out).astype(BF16)
        held = saved[:, h * LATENT : (h + 1) * LATENT]
        product = grads.astype(F32) * held.astype(F32)
        delta[:, span] = jnp.sum(product.T, axis=0, keepdims=True)
        weight_part[LATENT:, cols] = dot_tn(held, out).astype(BF16)

    def score(index, carry):
        span = pl.ds(pl.multiple_of(index * CHUNK, CHUNK), CHUNK)
        weights[span, :] = dot(keys[span, :], query_t[...])
        prob_grad[span, :] = dot(keys[span, :LATENT], grad_out_t[...])

        @pl.when(index == own // (CHUNK // TOK))
        def _():
            mine = pl.ds(pl.multiple_of(own * TOK, TOK), TOK)
            key_row = lax.broadcasted_iota(jnp.int32, (TOK, rows), 0)
            query_row = lax.rem(lax.broadcasted_iota(jnp.int32, (TOK, rows), 1), TOK)
            half = TOK // 2
            later = (key_row // half == query_row // half) & (key_row > query_row)
            weights[mine, :] = jnp.where(later, HIDDEN, weights[mine, :])

        raw = weights[span, :]
        top = jnp.max(raw, axis=0, keepdims=True)
        raised = jnp.exp2((raw - top) * log2_scale)
        weights[span, :] = raised
        tops[index] = top
        sums[index] = jnp.sum(raised, axis=0, keepdims=True)
        return carry

    lax.fori_loop(0, chunks, score, 0)
    highest = jnp.max(tops[...], axis=0)
    shares = jnp.exp2((tops[...] - highest[None]) * log2_scale)
    total = jnp.sum(shares * sums[...], axis=0)
    sums[...] = shares / total[None]
    query_grad[...] = jnp.zeros_like(query_grad)

    def grads(index, carry):
        span = pl.ds(pl.multiple_of(index * CHUNK, CHUNK), CHUNK)
        probs = weights[span, :] * sums[index]
        score_grad = (probs * (prob_grad[span, :] - delta[...]) * scale).astype(BF16)
        probs_low = probs.astype(BF16)
        latent_part[span, :] = (dot(score_grad, absorbed[...]) + dot(probs_low, grad_out[...])).astype(BF16)
        query_grad[...] += dot_tn(keys[span, :], score_grad)
        return carry

    lax.fori_loop(0, chunks, grads, 0)
    for h in range(heads):
        cols = slice(h * NOPE, (h + 1) * NOPE)
        span = slice(h * TOK, (h + 1) * TOK)
        absorbed_grad = query_grad[:LATENT, span].astype(BF16)
        weight_part[:LATENT, cols] = dot(absorbed_grad, query_nope[:, cols]).astype(BF16)
        grad_nope[:, cols] = dot_tn(absorbed_grad, key_weight[:, cols]).astype(BF16)
    rope_grad = jnp.concatenate(
        [query_grad[LATENT : LATENT + ROPE, h * TOK : (h + 1) * TOK] for h in range(heads)], axis=0
    )
    grad_rope[...] = rope_grad.T.astype(BF16)


def attention(owner, keys, query_nope, query_rope, key_weight, value_weight, saved, output_grad):
    total = keys.shape[0]
    heads = query_nope.shape[1] // NOPE
    rows = heads * TOK
    chunks = total // CHUNK
    vmem = pl.BlockSpec(memory_space=pltpu.VMEM)
    return pl.pallas_call(
        attention_kernel,
        out_shape=(
            jax.ShapeDtypeStruct(query_nope.shape, BF16),
            jax.ShapeDtypeStruct(query_rope.shape, BF16),
            jax.ShapeDtypeStruct((total, LATENT), BF16),
            jax.ShapeDtypeStruct((2 * LATENT, query_nope.shape[1]), BF16),
        ),
        in_specs=[pl.BlockSpec(memory_space=pltpu.SMEM)] + [vmem] * 7,
        out_specs=(vmem,) * 4,
        scratch_shapes=[
            pltpu.VMEM((WIDE, rows), BF16),
            pltpu.VMEM((rows, LATENT), BF16),
            pltpu.VMEM((LATENT, rows), BF16),
            pltpu.VMEM((rows, LATENT), BF16),
            pltpu.VMEM((1, rows), F32),
            pltpu.VMEM((total, rows), F32),
            pltpu.VMEM((total, rows), F32),
            pltpu.VMEM((chunks, 1, rows), F32),
            pltpu.VMEM((chunks, 1, rows), F32),
            pltpu.VMEM((WIDE, rows), F32),
        ],
        compiler_params=pltpu.CompilerParams(vmem_limit_bytes=VMEM_LIMIT),
        name="attention_grads",
    )(owner, keys, query_nope, query_rope, key_weight, value_weight, saved, output_grad)


def reduce_kernel(
    latent,
    weight,
    out_latent,
    out_key,
    out_value,
    core_buf,
    z_buf,
    y_buf,
    x_buf,
    w_buf,
    w_near,
    w_all,
    core_send,
    core_recv,
    z_send,
    z_recv,
    y_send,
    y_recv,
    x_send,
    x_recv,
    last_send,
    last_recv,
    w_send,
    w_recv,
    wn_send,
    wn_recv,
    wb_send,
    wb_recv,
    wg_send,
    wg_recv,
):
    y, zh, zl, x, core = place()
    turn = 1 - 2 * core
    z = 2 * zh + zl
    sibling = device(y, zh, zl, x, 1 - core)
    y_peers = [device(wrap(y + d, NY), zh, zl, x, core) for d in range(1, NY)]
    zh_peers = [device(y, wrap(zh + d, NZH), zl, x, core) for d in range(1, NZH)]
    x_peers = [device(y, zh, zl, wrap(x + d, NX), core) for d in range(1, NX)]
    across = [device(y, zh, 1 - zl, x, core), device(y, zh, 1 - zl, x, 1 - core)]

    def z_device(where):
        return device(y, where // 2, lax.rem(where, 2), x, core)

    ring_far = z_device(wrap(z - 1 + 2 * zl, NZ))
    y_next = device(wrap(y + turn, NY), zh, zl, x, core)
    z_next = z_device(wrap(z + turn, NZ))
    greet([sibling] + y_peers + zh_peers + x_peers + across + [ring_far])

    core_copies = []
    for step in range(NZ):
        where = wrap(z + turn * (step + 1), NZ)
        core_copies.append(
            copy_to(
                latent.at[:, where // 2, 1 - core, lax.rem(where, 2)],
                core_buf.at[step],
                core_send.at[step],
                core_recv.at[step],
                sibling,
            )
        )
        core_copies[-1].start()

    half_y = NY // 2

    def z_copy(step, sub):
        part = pl.ds(sub * half_y, half_y)
        return copy_to(
            core_buf.at[step, part], z_buf.at[step, part], z_send.at[step, sub], z_recv.at[step, sub], z_next
        )

    def latent_step(step, sub):
        part = pl.ds(sub * half_y, half_y)
        if sub == 0:
            core_copies[step].wait_recv()
        where = wrap(z - turn * (step + 1), NZ)
        if step > 0:
            z_copy(step - 1, sub).wait_recv()
        own = latent.at[:, where // 2, core, lax.rem(where, 2)]

        def add(index, carry):
            row = sub * half_y + index
            value = own[row].astype(F32) + core_buf[step, row].astype(F32)
            if step > 0:
                value += z_buf[step - 1, row].astype(F32)
            core_buf[step, row] = value.astype(BF16)
            return carry

        lax.fori_loop(0, half_y, add, 0)
        if step < NZ - 1:
            z_copy(step, sub).start()

    half_z = NZH // 2

    def w_copy(step, sub):
        part = pl.ds(sub * half_z, half_z)
        if step == 0:
            source = weight.at[wrap(y - turn, NY), part]
        else:
            source = w_buf.at[step - 1, part]
        return copy_to(source, w_buf.at[step, part], w_send.at[step, sub], w_recv.at[step, sub], y_next)

    def weight_start():
        for sub in range(2):
            w_copy(0, sub).start()

    def weight_step(step, sub):
        where = wrap(y - turn * (step + 2), NY)
        w_copy(step, sub).wait_recv()

        def add(index, carry):
            row = sub * half_z + index
            value = w_buf[step, row].astype(F32) + weight[where, row].astype(F32)
            w_buf[step, row] = value.astype(BF16)
            return carry

        lax.fori_loop(0, half_z, add, 0)
        if step + 1 < NY - 1:
            w_copy(step + 1, sub).start()

    def near_copy(d):
        target = wrap(zh + d, NZH)
        return copy_to(
            w_buf.at[NY - 2, target], w_near.at[d - 1], wn_send.at[d - 1], wn_recv.at[d - 1], zh_peers[d - 1]
        )

    def weight_near():
        for d in range(1, NZH):
            near_copy(d).start()

    def back_copy(d, source):
        region = w_all.at[y, source]
        return copy_to(region, region, wb_send.at[d - 1], wb_recv.at[d - 1], zh_peers[d - 1])

    def weight_sum():
        value = w_buf[NY - 2, zh].astype(F32)
        for d in range(1, NZH):
            near_copy(d).wait_recv()
            value += w_near[d - 1].astype(F32)
        w_all[y, zh] = value.astype(BF16)
        for d in range(1, NZH):
            back_copy(d, zh).start()

    def weight_collect():
        for d in range(1, NZH):
            back_copy(d, wrap(zh - d, NZH)).wait_recv()

    def spread_copy(step, sub, where):
        region = w_all.at[where, pl.ds(sub * half_z, half_z)]
        return copy_to(region, region, wg_send.at[step, sub], wg_recv.at[step, sub], y_next)

    def spread_start(step, sub):
        spread_copy(step, sub, wrap(y - turn * step, NY)).start()

    def spread_step(step, sub):
        spread_copy(step, sub, wrap(y - turn * (step + 1), NY)).wait_recv()
        if step + 1 < NY - 1:
            spread_start(step + 1, sub)

    weight_jobs = [weight_start]
    for step in range(NY - 1):
        for sub in range(2):
            weight_jobs.append(functools.partial(weight_step, step, sub))
    weight_jobs += [weight_near, weight_sum, weight_collect]
    weight_jobs.append(lambda: [spread_start(0, sub) for sub in range(2)])
    for step in range(NY - 1):
        for sub in range(2):
            weight_jobs.append(functools.partial(spread_step, step, sub))
    latent_jobs = []
    for step in range(NZ):
        for sub in range(2):
            latent_jobs.append(functools.partial(latent_step, step, sub))

    def y_copy(d):
        target = wrap(y + d, NY)
        return copy_to(
            core_buf.at[NZ - 1, target], y_buf.at[d - 1], y_send.at[d - 1], y_recv.at[d - 1], y_peers[d - 1]
        )

    def latent_y_start():
        for d in range(1, NY):
            y_copy(d).start()

    def x_copy(d, source):
        return copy_to(
            x_buf.at[source], x_buf.at[source], x_send.at[d - 1], x_recv.at[d - 1], x_peers[d - 1]
        )

    def latent_y_sum():
        value = core_buf[NZ - 1, y].astype(F32)
        for d in range(1, NY):
            y_copy(d).wait_recv()
            value += y_buf[d - 1].astype(F32)
        x_buf[x] = value.astype(BF16)
        for d in range(1, NX):
            x_copy(d, x).start()

    last_peers = [sibling] + across

    def last_copy(index, half, low):
        region = out_latent.at[half, low]
        return copy_to(region, region, last_send.at[index], last_recv.at[index], last_peers[index])

    def latent_x_sum():
        for d in range(1, NX):
            x_copy(d, wrap(x - d, NX)).wait_recv()
        value = x_buf[0].astype(F32)
        for index in range(1, NX):
            value += x_buf[index].astype(F32)
        out_latent[core, zl] = value.astype(BF16)
        for index in range(3):
            last_copy(index, core, zl).start()

    def latent_last():
        last_copy(0, 1 - core, zl).wait_recv()
        last_copy(1, core, 1 - zl).wait_recv()
        last_copy(2, 1 - core, 1 - zl).wait_recv()

    latent_jobs += [latent_y_start, latent_y_sum, latent_x_sum]

    done = 0
    for index, job in enumerate(weight_jobs):
        job()
        upto = (index + 1) * len(latent_jobs) // len(weight_jobs)
        while done < upto:
            latent_jobs[done]()
            done += 1

    for k in range(NY // 2):
        out_key[k] = w_all[k].astype(F32)
        out_value[k] = w_all[NY // 2 + k].astype(F32)
    latent_last()

    for copy in core_copies:
        copy.wait_send()
    for step in range(NZ - 1):
        for sub in range(2):
            z_copy(step, sub).wait_send()
    for step in range(NY - 1):
        for sub in range(2):
            w_copy(step, sub).wait_send()
            spread_copy(step, sub, wrap(y - turn * step, NY)).wait_send()
    for d in range(1, NY):
        y_copy(d).wait_send()
    for d in range(1, NX):
        x_copy(d, x).wait_send()
    for d in range(1, NZH):
        near_copy(d).wait_send()
        back_copy(d, zh).wait_send()
    for index in range(3):
        last_copy(index, core, zl).wait_send()


def reduce_grads(latent_part, weight_part):
    latent = latent_part.reshape(NY, NZH, 2, 2, 32, LATENT)
    wide = weight_part.shape[1]
    piece = 2 * LATENT // (NY * NZH)
    weight = weight_part.reshape(NY, NZH, piece, wide)
    vmem = pl.BlockSpec(memory_space=pltpu.VMEM)
    dma = pltpu.SemaphoreType.DMA
    pairs = lambda *shape: [dma(shape), dma(shape)]
    out = pl.pallas_call(
        reduce_kernel,
        out_shape=(
            jax.ShapeDtypeStruct((2, 2, 32, LATENT), BF16),
            jax.ShapeDtypeStruct((NY // 2, NZH, piece, wide), F32),
            jax.ShapeDtypeStruct((NY // 2, NZH, piece, wide), F32),
        ),
        in_specs=[vmem, vmem],
        out_specs=(vmem,) * 3,
        scratch_shapes=[
            pltpu.VMEM((NZ, NY, 32, LATENT), BF16),
            pltpu.VMEM((NZ - 1, NY, 32, LATENT), BF16),
            pltpu.VMEM((NY - 1, 32, LATENT), BF16),
            pltpu.VMEM((NX, 32, LATENT), BF16),
            pltpu.VMEM((NY - 1, NZH, piece, wide), BF16),
            pltpu.VMEM((NZH - 1, piece, wide), BF16),
            pltpu.VMEM((NY, NZH, piece, wide), BF16),
        ]
        + pairs(NZ)
        + pairs(NZ - 1, 2)
        + pairs(NY - 1)
        + pairs(NX - 1)
        + pairs(3)
        + pairs(NY - 1, 2)
        + pairs(NZH - 1)
        + pairs(NZH - 1)
        + pairs(NY - 1, 2),
        compiler_params=pltpu.CompilerParams(
            collective_id=1, has_side_effects=True, vmem_limit_bytes=VMEM_LIMIT
        ),
        name="reduce_grads",
    )(latent, weight)
    return (
        out[0].reshape(4 * 32, LATENT),
        out[1].reshape(LATENT, wide),
        out[2].reshape(LATENT, wide),
    )


def on_device(
    block_owner,
    query_nope,
    query_rope,
    latent_cache,
    key_up_weight,
    value_up_weight,
    saved_output,
    output_grad,
):
    keys = gather_keys(block_owner, latent_cache).reshape(NY * NZH * TOK, WIDE)
    grad_nope, grad_rope, latent_part, weight_part = attention(
        block_owner, keys, query_nope, query_rope, key_up_weight, value_up_weight, saved_output, output_grad
    )
    grad_latent, grad_key, grad_value = reduce_grads(latent_part, weight_part)
    return grad_nope, grad_rope, grad_latent, grad_key, grad_value


def solution(mesh):
    return jax.shard_map(
        on_device,
        mesh=mesh,
        in_specs=(
            P("ctx"),
            P("ctx", "head"),
            P("ctx", "head"),
            P("ctx", None),
            P(None, "head"),
            P(None, "head"),
            P("ctx", "head"),
            P("ctx", "head"),
        ),
        out_specs=(
            P("ctx", "head"),
            P("ctx", "head"),
            P("ctx", None),
            P(None, "head"),
            P(None, "head"),
        ),
        check_vma=False,
    )
```

time: 930 us -> 167 us (0.18)
  waiting for transfers between devices: 704 us -> 0 us
  Pallas kernels: 0 us -> 158 us
  blocking collectives: 73.7 us -> 0 us
  matrix products: 64.6 us -> 0 us
  local copies, waits for them, and re-layouts: 30.2 us -> 7.81 us
  loops' own time: 21.4 us -> 0 us
  other arithmetic: 19.9 us -> 0 us
  between operations: 14 us -> 0.65 us
    psum x2 -> x0, waiting for transfers between devices: 445 us -> none  [the longest x1 304 us: on_device(): lax.psum(key_part.astype(jnp.bfloat16), 'ctx').astype(jnp.float32)]
    reduce_scatter x1 -> x0, waiting for transfers between devices: 223 us -> none  [on_device(): lax.psum_scatter(grad_result[1].astype(jnp.bfloat16), 'ctx', scatter_dime...]
    pallas_call x0 -> x3, Pallas kernels: none -> 158 us  [the longest x1 81.5 us: reduce_grads(): pl.pallas_call(reduce_kernel, out_shape=(jax.ShapeDtypeStruct((2, 2, 32,...]
    all_gather x1 -> x0, blocking collectives: 73.7 us -> none  [on_device(): lax.all_gather(local_positions, 'ctx', axis=0, tiled=True)]
    dot_general x53 -> x0, matrix products: 64.6 us -> none  [the longest x16 29.8 us: masked_scores(): jnp.einsum('rf,kf->rk', queries, key_rows, preferred_element_type=jnp.flo...]
    all_gather x1 -> x0, waiting for transfers between devices: 35.9 us -> none  [on_device(): lax.all_gather(latent_cache, 'ctx', axis=0, tiled=True)]
    another operation x18 -> x0, loops' own time: 21.4 us -> none  [the longest x2 20.8 us: sweep_blocks(): return lax.fori_loop(0, block_turns, block_turn, carried)]
    reduce_min x16 -> x0, other arithmetic: 12 us -> none  [the longest x8 6.16 us: stat_step(): jnp.min(key_positions) <= latest_query]
  transfers between devices with their start and end apart: 4 -> 0, of which waited for: 4 -> 0; matrix products, arithmetic and copies ran while one was open for 2% -> 0% of each run, Pallas kernels for 0% -> 0%
where the time goes in v1:
time: 167 us
  Pallas kernels  158 us (95%)
  local copies, waits for them, and re-layouts  7.81 us (5%)
    pallas_call x1, Pallas kernels, reduce_grads(): pl.pallas_call(reduce_kernel, out_shape=(jax.ShapeDtypeStruct((2, 2, 32,...  81.5 us
    pallas_call x1, Pallas kernels, gather_keys(): pl.pallas_call(gather_kernel, out_shape=jax.ShapeDtypeStruct((NY, NZH, 2,...  53 us
    pallas_call x1, Pallas kernels, attention(): pl.pallas_call(attention_kernel, out_shape=(jax.ShapeDtypeStruct(query_no...  23.9 us
    unnamed x4, local copies, waits for them, and re-layouts  7.81 us

profile of v1, /device:TPU:1, one launch (start us, length us, event | category | flops | bytes accessed | tf_op | source)
XLA Modules:
  0.0 166.9 jit_solution(1643694209791567809)
XLA Ops:
  0.6 1.7 %copy.13.latent = bf16[128,576]{1,0:T(8,128)(2,1)} copy(bf16[128,576]{0,1:T(8,128)(2,1)} %param.11) | data formatting | bytes 294912 | tf_op args[3]
  2.3 53.0 %gather_keys.1 = bf16[8,4,2,2,2,16,640]{6,5,4,3,2,1,0:T(8,128)(2,1)} custom-call(s32[2]{0:T(128)} %owner.3, bf16[128,576]{1,0:T(8,128)(2,1)} %copy.13.latent), custom_call_target="tpu_custom_call" | custom-call | tf_op jit(solution)/shard_map/gather_keys/pallas_call | solution.py:190
  55.3 23.9 %attention_grads.1 = (bf16[128,512]{1,0:T(8,128)(2,1)}, bf16[128,256]{1,0:T(8,128)(2,1)}, bf16[4096,512]{1,0:T(8,128)(2,1)}, bf16[1024,512]{1,0:T(8,128)(2,1)}) custom-call(s32[2]{0:T(128)} %owner.3, bf16[4096,640]{1,0:T(8,128)(2,1)} %bitcast.6, bf16[128,512]{1,0:T(8,128)(2,1)} %query_nope.1, bf16[128,256]{1,0:T(8,128)(2,1)} %query_rope.1, ...), custom_call_target="tpu_custom_call" | custom-call | tf_op jit(solution)/shard_map/attention_grads/pallas_call | solution.py:337
  79.3 81.5 %reduce_grads.1 = (bf16[2,2,32,512]{3,2,1,0:T(8,128)(2,1)}, f32[4,4,32,512]{3,2,1,0:T(8,128)}, f32[4,4,32,512]{3,2,1,0:T(8,128)}) custom-call(bf16[8,4,2,2,32,512]{5,4,3,2,1,0:T(8,128)(2,1)} %bitcast.7, bf16[8,4,32,512]{3,2,1,0:T(8,128)(2,1)} %bitcast.8), custom_call_target="tpu_custom_call" | custom-call | tf_op jit(solution)/shard_map/reduce_grads/pallas_call | solution.py:625
  160.8 1.6 copy.17
  162.4 2.3 %copy.18 = f32[512,512]{1,0:T(8,128)} copy(f32[512,512]{1,0:T(8,128)} %bitcast.10) | data formatting | bytes 2097152
  164.6 2.3 %copy.19 = f32[512,512]{1,0:T(8,128)} copy(f32[512,512]{1,0:T(8,128)} %bitcast.9) | data formatting | bytes 2097152

commit v2 on v0

v2 whole, which is shorter than its diff:
```python
import math

import jax
import jax.numpy as jnp
from jax import lax
from jax.experimental import pallas as pl
from jax.experimental.pallas import tpu as pltpu
from jax.sharding import PartitionSpec as P

LATENT = 512
ROPE = 64
NOPE = 128
NY, NZH, NX = 8, 4, 4
NZ = 2 * NZH
BLOCKS = 64
WIDE = LATENT + ROPE + BLOCKS
TOK = 128
GROUPS = 4
HIDDEN = -1e30
BF16 = jnp.bfloat16
F32 = jnp.float32
VMEM_LIMIT = 60 * 1024 * 1024


def device(y, zh, zl, x, core):
    return (y * NZH + zh, zl * (2 * NX) + x * 2 + core)


def copy_to(src, dst, send_sem, recv_sem, target):
    return pltpu.make_async_remote_copy(
        src_ref=src,
        dst_ref=dst,
        send_sem=send_sem,
        recv_sem=recv_sem,
        device_id=target,
        device_id_type=pl.DeviceIdType.MESH,
    )


def wrap(index, size):
    return lax.rem(index + 2 * size, size)


def each(start, stop, body):
    def step(index, carry):
        body(index)
        return carry

    lax.fori_loop(start, stop, step, 0)


def rows(start, size, step=16):
    return pl.ds(pl.multiple_of(start, step), size)


def dot(left, right):
    return jnp.dot(left, right, preferred_element_type=F32)


def dot_nt(left, right):
    return lax.dot_general(left, right, (((1,), (1,)), ((), ())), preferred_element_type=F32)


def dot_tn(left, right):
    return lax.dot_general(left, right, (((0,), (0,)), ((), ())), preferred_element_type=F32)


def fused_kernel(
    owner,
    latent,
    query_nope,
    query_rope,
    key_weight,
    value_weight,
    saved,
    output_grad,
    grad_nope,
    grad_rope,
    weight_all,
    latent_out,
    keys,
    query_t,
    absorbed,
    grad_out_t,
    grad_out,
    delta,
    weights,
    prob_grad,
    score_low,
    probs_low,
    tops,
    sums,
    query_grad,
    weight_part,
    wa_in,
    wb_in,
    wa_sum,
    wb_sum,
    wa_near,
    wb_near,
    part,
    pair,
    ring,
    mine,
    y_in,
    z_in,
    y_sum,
    z_sum,
    y_last,
    z_last,
    near_y_send,
    near_y_recv,
    near_z_send,
    near_z_recv,
    ring_send,
    ring_recv,
    pass_send,
    pass_recv,
    wy_send,
    wy_recv,
    wz_send,
    wz_recv,
    pair_send,
    pair_recv,
    x_send,
    x_recv,
    ly_send,
    ly_recv,
    lz_send,
    lz_recv,
    head_send,
    head_recv,
):
    heads = query_nope.shape[1] // NOPE
    count = heads * TOK
    scale = (NOPE + ROPE) ** -0.5
    log2_scale = scale * math.log2(math.e)
    half = keys.shape[1] // 2
    chunks = keys.shape[0]

    ctx, head = lax.axis_index("ctx"), lax.axis_index("head")
    y, zh = ctx // NZH, lax.rem(ctx, NZH)
    zl = head // (2 * NX)
    x = lax.rem(head // 2, NX)
    core = lax.rem(head, 2)
    z = 2 * zh + zl
    turn = 1 - 2 * core
    sibling = device(y, zh, zl, x, 1 - core)
    heads_all = 4 * NX

    def y_peer(where):
        return device(where, zh, zl, x, core)

    def z_peer(where):
        return device(y, where // 2, lax.rem(where, 2), x, core)

    def zh_peer(where):
        return device(y, where, zl, x, core)

    def x_peer(where):
        return device(y, zh, zl, where, core)

    column = lax.broadcasted_iota(jnp.int32, (16, BLOCKS), 1)
    for side in range(2):
        mark = jnp.where(column == owner[side], 1.0, 0.0).astype(BF16)
        for piece in range(4):
            start = side * 64 + piece * 16
            if piece < 2:
                where, spot = y, rows(side * half + zh * 32 + piece * 16, 16)
            else:
                where, spot = NY + 2 * zh + piece - 2, rows(side * half + y * 16, 16)
            keys[where, spot, : LATENT + ROPE] = latent[start : start + 16, :]
            keys[where, spot, LATENT + ROPE :] = mark

    barrier = pltpu.get_barrier_semaphore()

    def hail(target):
        pl.semaphore_signal(barrier, inc=1, device_id=target, device_id_type=pl.DeviceIdType.MESH)

    each(1, NY, lambda d: hail(y_peer(wrap(y + d, NY))))
    each(1, NZ, lambda d: hail(z_peer(wrap(z + d, NZ))))
    each(1, heads_all, lambda d: hail((ctx, wrap(head + d, heads_all))))
    pl.semaphore_wait(barrier, NY - 1 + NZ - 1 + heads_all - 1)

    def near_y(d, spot):
        region = keys.at[NY + z, rows(core * half + spot * 16, 16)]
        return copy_to(region, region, near_y_send.at[d - 1], near_y_recv.at[d - 1], y_peer(wrap(y + d, NY)))

    def near_z(d, spot):
        region = keys.at[y, rows(core * half + spot * 32, 32, 32)]
        return copy_to(region, region, near_z_send.at[d - 1], near_z_recv.at[d - 1], zh_peer(wrap(zh + d, NZH)))

    each(1, NZH, lambda d: near_z(d, zh).start())
    each(1, NY, lambda d: near_y(d, y).start())

    rope_t = query_rope[...].astype(F32).T.astype(BF16)
    block = lax.broadcasted_iota(jnp.int32, (BLOCKS, TOK), 0)
    token = lax.broadcasted_iota(jnp.int32, (BLOCKS, TOK), 1)
    limit = jnp.where(token < TOK // 2, owner[0], owner[1])
    bias = jnp.where(block <= limit, 0.0, HIDDEN).astype(BF16)
    for h in range(heads):
        cols = slice(h * NOPE, (h + 1) * NOPE)
        span = slice(h * TOK, (h + 1) * TOK)
        query, weight = query_nope[:, cols], key_weight[:, cols]
        query_t[:LATENT, span] = dot_nt(weight, query).astype(BF16)
        query_t[LATENT : LATENT + ROPE, span] = rope_t[h * ROPE : (h + 1) * ROPE, :]
        query_t[LATENT + ROPE :, span] = bias
        grad_out_t[:, span] = dot_nt(value_weight[:, cols], output_grad[:, cols]).astype(BF16)

    places = ((y, NY, 0), (z, NZ, NY))

    def ring_target(axis, rel):
        way = turn if rel == 0 else -turn
        return y_peer(wrap(y + way, NY)) if axis == 0 else z_peer(wrap(z + way, NZ))

    def ring_chunk(axis, rel, step):
        at, size, base = places[axis]
        way = turn if rel == 0 else -turn
        return base + wrap(at - way * step, size)

    def ring_copy(axis, rel, step, where):
        region = keys.at[where, rows(core * half, half, half)]
        return copy_to(
            region, region, ring_send.at[axis, rel, step], ring_recv.at[axis, rel, step], ring_target(axis, rel)
        )

    def pass_copy(axis, slot, where, side):
        region = keys.at[where, rows(side * half, half, half)]
        return copy_to(region, region, pass_send.at[axis, slot], pass_recv.at[axis, slot], sibling)

    def score(where):
        rows_in = keys[where]
        weights[where] = dot(rows_in, query_t[...])
        prob_grad[where] = dot(rows_in[:, :LATENT], grad_out_t[...])

        def hide(first, size, offset):
            for side in range(2):
                spot = rows(side * half + first, size)
                key_row = lax.broadcasted_iota(jnp.int32, (size, count), 0) + offset
                query_row = lax.rem(lax.broadcasted_iota(jnp.int32, (size, count), 1), TOK) - side * 64
                later = (query_row >= 0) & (query_row < 64) & (key_row > query_row)
                weights[where, spot, :] = jnp.where(later, HIDDEN, weights[where, spot, :])

        @pl.when(where == y)
        def _():
            hide(zh * 32, 32, 0)

        low = where - NY - 2 * zh

        @pl.when((low >= 0) & (low < 2))
        def _():
            hide(y * 16, 16, 32 + low * 16)

        raw = weights[where]
        top = jnp.max(raw, axis=0, keepdims=True)
        raised = jnp.exp2((raw - top) * log2_scale)
        weights[where] = raised
        tops[where] = top
        sums[where] = jnp.sum(raised, axis=0, keepdims=True)

    each(1, NZH, lambda d: near_z(d, wrap(zh - d, NZH)).wait_recv())
    for rel in range(2):
        if rel == 0 or NY > 2:
            ring_copy(0, rel, 0, y).start()
    each(1, NY, lambda d: near_y(d, wrap(y - d, NY)).wait_recv())
    for rel in range(2):
        if rel == 0 or NZ > 2:
            ring_copy(1, rel, 0, NY + z).start()
    pass_copy(0, 0, y, core).start()
    pass_copy(1, 0, NY + z, core).start()

    for h in range(heads):
        cols = slice(h * NOPE, (h + 1) * NOPE)
        span = slice(h * TOK, (h + 1) * TOK)
        side, at = h // (heads // 2), h % (heads // 2)
        place = slice(at * NOPE, (at + 1) * NOPE)
        out = output_grad[:, cols]
        grads = dot_nt(out, value_weight[:, cols]).astype(BF16)
        grad_out[span, :] = grads
        held = saved[:, h * LATENT : (h + 1) * LATENT]
        product = grads.astype(F32) * held.astype(F32)
        delta[:, span] = jnp.sum(product.T, axis=0, keepdims=True)
        weight_part[0, side, :, place] = dot_tn(held, out).astype(BF16)
        absorbed[span, :] = dot_nt(query_nope[:, cols], key_weight[:, cols]).astype(BF16)

    pass_copy(0, 0, y, 1 - core).wait_recv()
    pass_copy(1, 0, NY + z, 1 - core).wait_recv()
    each(0, 2, lambda i: score(i * (NY + z) + (1 - i) * y))

    ra, rb, rp = LATENT // NY, LATENT // NZH, LATENT // (NY * NZH)

    def wy_copy(w, stage, d, src, dst):
        return copy_to(
            src, dst, wy_send.at[w, stage, d - 1], wy_recv.at[w, stage, d - 1], y_peer(wrap(y + d, NY))
        )

    def wz_copy(w, stage, d, src, dst):
        return copy_to(
            src, dst, wz_send.at[w, stage, d - 1], wz_recv.at[w, stage, d - 1], zh_peer(wrap(zh + d, NZH))
        )

    def a_first(w, d):
        return wy_copy(w, 0, d, weight_part.at[w, 0, rows(wrap(y + d, NY) * ra, ra)], wa_in.at[w, d - 1])

    def b_first(w, d):
        return wz_copy(w, 0, d, weight_part.at[w, 1, rows(wrap(zh + d, NZH) * rb, rb)], wb_in.at[w, d - 1])

    def a_second(w, d):
        return wz_copy(w, 1, d, wa_sum.at[w, rows(wrap(zh + d, NZH) * rp, rp)], wa_near.at[w, d - 1])

    def b_second(w, d):
        return wy_copy(w, 1, d, wb_sum.at[w, rows(wrap(y + d, NY) * rp, rp)], wb_near.at[w, d - 1])

    def a_third(w, d, where):
        region = weight_all.at[w, 0, rows(y * ra + where * rp, rp)]
        return wz_copy(w, 2, d, region, region)

    def b_third(w, d, where):
        region = weight_all.at[w, 1, rows(zh * rb + where * rp, rp)]
        return wy_copy(w, 2, d, region, region)

    def a_fourth(w, d, where):
        region = weight_all.at[w, 0, rows(where * ra, ra)]
        return wy_copy(w, 3, d, region, region)

    def b_fourth(w, d, where):
        region = weight_all.at[w, 1, rows(where * rb, rb)]
        return wz_copy(w, 3, d, region, region)

    def weight_first(w):
        each(1, NY, lambda d: a_first(w, d).start())
        each(1, NZH, lambda d: b_first(w, d).start())

    def weight_second(w):
        each(1, NY, lambda d: a_first(w, d).wait_recv())
        total = weight_part[w, 0, rows(y * ra, ra), :].astype(F32)
        for d in range(1, NY):
            total += wa_in[w, d - 1].astype(F32)
        wa_sum[w] = total.astype(BF16)
        each(1, NZH, lambda d: a_second(w, d).start())
        each(1, NZH, lambda d: b_first(w, d).wait_recv())
        total = weight_part[w, 1, rows(zh * rb, rb), :].astype(F32)
        for d in range(1, NZH):
            total += wb_in[w, d - 1].astype(F32)
        wb_sum[w] = total.astype(BF16)
        each(1, NY, lambda d: b_second(w, d).start())

    def weight_third(w):
        each(1, NZH, lambda d: a_second(w, d).wait_recv())
        total = wa_sum[w, rows(zh * rp, rp), :].astype(F32)
        for d in range(1, NZH):
            total += wa_near[w, d - 1].astype(F32)
        weight_all[w, 0, rows(y * ra + zh * rp, rp), :] = total.astype(BF16)
        each(1, NZH, lambda d: a_third(w, d, zh).start())
        each(1, NY, lambda d: b_second(w, d).wait_recv())
        total = wb_sum[w, rows(y * rp, rp), :].astype(F32)
        for d in range(1, NY):
            total += wb_near[w, d - 1].astype(F32)
        weight_all[w, 1, rows(zh * rb + y * rp, rp), :] = total.astype(BF16)
        each(1, NY, lambda d: b_third(w, d, y).start())

    def weight_fourth(w):
        each(1, NZH, lambda d: a_third(w, d, wrap(zh - d, NZH)).wait_recv())
        each(1, NY, lambda d: a_fourth(w, d, y).start())
        each(1, NY, lambda d: b_third(w, d, wrap(y - d, NY)).wait_recv())
        each(1, NZH, lambda d: b_fourth(w, d, zh).start())

    def weight_last(w):
        each(1, NY, lambda d: a_fourth(w, d, wrap(y - d, NY)).wait_recv())
        each(1, NZH, lambda d: b_fourth(w, d, wrap(zh - d, NZH)).wait_recv())

    def weight_sent(w):
        def over_y(d):
            a_first(w, d).wait_send()
            b_second(w, d).wait_send()
            b_third(w, d, y).wait_send()
            a_fourth(w, d, y).wait_send()

        def over_z(d):
            b_first(w, d).wait_send()
            a_second(w, d).wait_send()
            a_third(w, d, zh).wait_send()
            b_fourth(w, d, zh).wait_send()

        each(1, NY, over_y)
        each(1, NZH, over_z)

    last = NY // 2 - 1
    for step in range(last):
        for rel in range(2):
            for axis in range(2):
                where = ring_chunk(axis, rel, step + 1)
                ring_copy(axis, rel, step, where).wait_recv()
                if rel == 0 or step + 1 < last:
                    ring_copy(axis, rel, step + 1, where).start()
                pass_copy(axis, 1 + 2 * step + rel, where, core).start()
        for rel in range(2):
            for axis in range(2):
                where = ring_chunk(axis, 1 - rel, step + 1)
                pass_copy(axis, 1 + 2 * step + rel, where, 1 - core).wait_recv()

        def arrived(i):
            axis, sign = i // 2, 1 - 2 * lax.rem(i, 2)
            score((1 - axis) * wrap(y - sign * (step + 1), NY) + axis * (NY + wrap(z - sign * (step + 1), NZ)))

        each(0, 4, arrived)
    for axis in range(2):
        where = ring_chunk(axis, 0, last + 1)
        ring_copy(axis, 0, last, where).wait_recv()
        pass_copy(axis, 1 + 2 * last, where, core).start()
    weight_first(0)
    for axis in range(2):
        pass_copy(axis, 1 + 2 * last, ring_chunk(axis, 0, last + 1), 1 - core).wait_recv()
    each(0, 2, lambda i: score((1 - i) * wrap(y + last + 1, NY) + i * (NY + wrap(z + last + 1, NZ))))

    highest = jnp.max(tops[...], axis=0)
    shares = jnp.exp2((tops[...] - highest[None]) * log2_scale)
    total = jnp.sum(shares * sums[...], axis=0)
    sums[...] = shares / total[None]
    query_grad[...] = jnp.zeros_like(query_grad)

    def gradients(where):
        probs = weights[where] * sums[where]
        grads = (probs * (prob_grad[where] - delta[...]) * scale).astype(BF16)
        score_low[where] = grads
        probs_low[where] = probs.astype(BF16)
        query_grad[...] += dot_tn(keys[where], grads)

    each(0, chunks // 2, gradients)
    weight_second(0)
    each(chunks // 2, chunks, gradients)
    weight_third(0)
    for h in range(heads):
        cols = slice(h * NOPE, (h + 1) * NOPE)
        span = slice(h * TOK, (h + 1) * TOK)
        side, at = h // (heads // 2), h % (heads // 2)
        place = slice(at * NOPE, (at + 1) * NOPE)
        weight_part[1, side, :, place] = dot(query_grad[:LATENT, span].astype(BF16), query_nope[:, cols]).astype(BF16)
    weight_first(1)

    wide = LATENT // NX
    size = chunks // GROUPS
    x_next, x_back = x_peer(wrap(x + turn, NX)), x_peer(wrap(x - turn, NX))

    def pair_copy(g):
        group = pl.ds(g * size, size)
        return copy_to(
            part.at[:, group, rows((1 - core) * half, half, half)],
            pair.at[:, group],
            pair_send.at[g],
            pair_recv.at[g],
            sibling,
        )

    def x_copy(kind, g):
        group = pl.ds(g * size, size)
        target = x_back if kind == 1 else x_next
        where = wrap(x + 2, NX) if kind == 0 else wrap(x - turn, NX) if kind == 1 else wrap(x + turn, NX)
        return copy_to(
            pair.at[where, group], ring.at[kind, group], x_send.at[kind, g], x_recv.at[kind, g], target
        )

    def terms(g):
        def one(i):
            where = g * size + i
            value = dot(score_low[where], absorbed[...]) + dot(probs_low[where], grad_out[...])
            for k in range(NX):
                part[k, where] = value[:, k * wide : (k + 1) * wide].astype(BF16)

        each(0, size, one)
        pair_copy(g).start()

    def pair_sum(g):
        pair_copy(g).wait_recv()

        def one(i):
            where = g * size + i
            for k in range(NX):
                value = part[k, where, rows(core * half, half, half), :].astype(F32) + pair[k, where].astype(F32)
                pair[k, where] = value.astype(BF16)

        each(0, size, one)
        x_copy(0, g).start()
        x_copy(1, g).start()

    def x_sum(g):
        x_copy(0, g).wait_recv()
        to = wrap(x + turn, NX)

        def one(i):
            where = g * size + i
            pair[to, where] = (pair[to, where].astype(F32) + ring[0, where].astype(F32)).astype(BF16)

        each(0, size, one)
        x_copy(2, g).start()

    def x_last(g):
        x_copy(1, g).wait_recv()
        x_copy(2, g).wait_recv()

        def one(i):
            where = g * size + i
            value = pair[x, where].astype(F32) + ring[1, where].astype(F32) + ring[2, where].astype(F32)
            mine[where] = value.astype(BF16)

        each(0, size, one)

    terms(0)
    weight_fourth(0)
    terms(1)
    pair_sum(0)
    weight_second(1)
    terms(2)
    pair_sum(1)
    x_sum(0)
    terms(3)
    pair_sum(2)
    weight_third(1)
    x_sum(1)
    x_last(0)
    pair_sum(3)
    weight_fourth(1)
    x_sum(2)
    x_last(1)
    for h in range(heads):
        cols = slice(h * NOPE, (h + 1) * NOPE)
        span = slice(h * TOK, (h + 1) * TOK)
        grad_nope[:, cols] = dot_tn(query_grad[:LATENT, span].astype(BF16), key_weight[:, cols]).astype(BF16)
    x_sum(3)
    x_last(2)
    rope_grad = jnp.concatenate(
        [query_grad[LATENT : LATENT + ROPE, h * TOK : (h + 1) * TOK] for h in range(heads)], axis=0
    )
    grad_rope[...] = rope_grad.T.astype(BF16)
    x_last(3)

    def ly_copy(stage, d, src, dst):
        return copy_to(src, dst, ly_send.at[stage, d - 1], ly_recv.at[stage, d - 1], y_peer(wrap(y + d, NY)))

    def lz_copy(stage, d, src, dst):
        return copy_to(src, dst, lz_send.at[stage, d - 1], lz_recv.at[stage, d - 1], z_peer(wrap(z + d, NZ)))

    def y_first(d):
        return ly_copy(0, d, mine.at[wrap(y + d, NY)], y_in.at[d - 1])

    def z_first(d):
        return lz_copy(0, d, mine.at[NY + wrap(z + d, NZ)], z_in.at[d - 1])

    def y_second(d):
        return ly_copy(1, d, z_sum.at[rows(wrap(y + d, NY) * 16, 16)], y_last.at[d - 1])

    def z_second(d):
        return lz_copy(1, d, y_sum.at[rows(wrap(z + d, NZ) * 16, 16)], z_last.at[d - 1])

    each(1, NY, lambda d: y_first(d).start())
    each(1, NZ, lambda d: z_first(d).start())
    weight_last(0)
    each(1, NY, lambda d: y_first(d).wait_recv())
    total = mine[y].astype(F32)
    for d in range(1, NY):
        total += y_in[d - 1].astype(F32)
    y_sum[...] = total.astype(BF16)
    each(1, NZ, lambda d: z_second(d).start())
    each(1, NZ, lambda d: z_first(d).wait_recv())
    total = mine[NY + z].astype(F32)
    for d in range(1, NZ):
        total += z_in[d - 1].astype(F32)
    z_sum[...] = total.astype(BF16)
    each(1, NY, lambda d: y_second(d).start())

    def head_copy(d, who):
        region = latent_out.at[lax.rem(who, 2), who // (2 * NX), lax.rem(who // 2, NX)]
        return copy_to(
            region, region, head_send.at[d - 1], head_recv.at[d - 1], (ctx, wrap(head + d, heads_all))
        )

    each(1, NZ, lambda d: z_second(d).wait_recv())
    total = y_sum[rows(z * 16, 16), :].astype(F32)
    for d in range(1, NZ):
        total += z_last[d - 1].astype(F32)
    latent_out[core, zl, x, 0] = total.astype(BF16)
    each(1, NY, lambda d: y_second(d).wait_recv())
    total = z_sum[rows(y * 16, 16), :].astype(F32)
    for d in range(1, NY):
        total += y_last[d - 1].astype(F32)
    latent_out[core, zl, x, 1] = total.astype(BF16)
    each(1, heads_all, lambda d: head_copy(d, head).start())

    weight_last(1)
    each(1, NZH, lambda d: near_z(d, zh).wait_send())
    each(1, NY, lambda d: near_y(d, y).wait_send())
    for axis in range(2):
        for rel in range(2):
            for step in range(last + 1 - rel):
                ring_copy(axis, rel, step, ring_chunk(axis, rel, step)).wait_send()
        pass_copy(axis, 0, y if axis == 0 else NY + z, core).wait_send()
        for step in range(last + 1):
            for rel in range(2 if step < last else 1):
                pass_copy(axis, 1 + 2 * step + rel, ring_chunk(axis, rel, step + 1), core).wait_send()
    weight_sent(0)
    weight_sent(1)
    for g in range(GROUPS):
        pair_copy(g).wait_send()
        for kind in range(3):
            x_copy(kind, g).wait_send()

    def sent_y(d):
        y_first(d).wait_send()
        y_second(d).wait_send()

    def sent_z(d):
        z_first(d).wait_send()
        z_second(d).wait_send()

    each(1, NY, sent_y)
    each(1, NZ, sent_z)
    each(1, heads_all, lambda d: head_copy(d, wrap(head - d, heads_all)).wait_recv())
    each(1, heads_all, lambda d: head_copy(d, head).wait_send())


def fused(owner, latent, query_nope, query_rope, key_weight, value_weight, saved, output_grad):
    heads = query_nope.shape[1] // NOPE
    count = heads * TOK
    half = NZH * 32
    chunks = NY + NZ
    wide = LATENT // NX
    cols = count // 2
    ra, rb, rp = LATENT // NY, LATENT // NZH, LATENT // (NY * NZH)
    vmem = pl.BlockSpec(memory_space=pltpu.VMEM)
    dma = pltpu.SemaphoreType.DMA
    hold = pltpu.VMEM

    def sems(*shape):
        return [dma(shape), dma(shape)]

    return pl.pallas_call(
        fused_kernel,
        out_shape=(
            jax.ShapeDtypeStruct(query_nope.shape, BF16),
            jax.ShapeDtypeStruct(query_rope.shape, BF16),
            jax.ShapeDtypeStruct((2, 2, LATENT, cols), BF16),
            jax.ShapeDtypeStruct((2, 2, NX, 2, 16, wide), BF16),
        ),
        in_specs=[pl.BlockSpec(memory_space=pltpu.SMEM)] + [vmem] * 7,
        out_specs=(vmem,) * 4,
        scratch_shapes=[
            hold((chunks, 2 * half, WIDE), BF16),
            hold((WIDE, count), BF16),
            hold((count, LATENT), BF16),
            hold((LATENT, count), BF16),
            hold((count, LATENT), BF16),
            hold((1, count), F32),
            hold((chunks, 2 * half, count), F32),
            hold((chunks, 2 * half, count), F32),
            hold((chunks, 2 * half, count), BF16),
            hold((chunks, 2 * half, count), BF16),
            hold((chunks, 1, count), F32),
            hold((chunks, 1, count), F32),
            hold((WIDE, count), F32),
            hold((2, 2, LATENT, cols), BF16),
            hold((2, NY - 1, ra, cols), BF16),
            hold((2, NZH - 1, rb, cols), BF16),
            hold((2, ra, cols), BF16),
            hold((2, rb, cols), BF16),
            hold((2, NZH - 1, rp, cols), BF16),
            hold((2, NY - 1, rp, cols), BF16),
            hold((NX, chunks, 2 * half, wide), BF16),
            hold((NX, chunks, half, wide), BF16),
            hold((3, chunks, half, wide), BF16),
            hold((chunks, half, wide), BF16),
            hold((NY - 1, half, wide), BF16),
            hold((NZ - 1, half, wide), BF16),
            hold((half, wide), BF16),
            hold((half, wide), BF16),
            hold((NY - 1, 16, wide), BF16),
            hold((NZ - 1, 16, wide), BF16),
        ]
        + sems(NY - 1)
        + sems(NZH - 1)
        + sems(2, 2, NY // 2)
        + sems(2, NY)
        + sems(2, 4, NY - 1)
        + sems(2, 4, NZH - 1)
        + sems(GROUPS)
        + sems(3, GROUPS)
        + sems(2, NY - 1)
        + sems(2, NZ - 1)
        + sems(4 * NX - 1),
        compiler_params=pltpu.CompilerParams(
            collective_id=0, has_side_effects=True, vmem_limit_bytes=VMEM_LIMIT
        ),
        name="fused_grads",
    )(owner, latent, query_nope, query_rope, key_weight, value_weight, saved, output_grad)


def finish_kernel(nope, rope, weight, latent, grad_nope, grad_rope, grad_latent, grad_key, grad_value):
    grad_nope[...] = nope[...]
    grad_rope[...] = rope[...]
    wide = LATENT // NX
    cols = weight.shape[3]
    for core in range(2):
        for low in range(2):
            for x in range(NX):
                for kind in range(2):
                    start = core * 64 + kind * 32 + low * 16
                    grad_latent[start : start + 16, x * wide : (x + 1) * wide] = latent[core, low, x, kind]
    for side in range(2):
        grad_value[:, side * cols : (side + 1) * cols] = weight[0, side].astype(F32)
        grad_key[:, side * cols : (side + 1) * cols] = weight[1, side].astype(F32)


def finish(nope, rope, weight, latent):
    vmem = pl.BlockSpec(memory_space=pltpu.VMEM)
    cols = 2 * weight.shape[3]
    return pl.pallas_call(
        finish_kernel,
        out_shape=(
            jax.ShapeDtypeStruct(nope.shape, BF16),
            jax.ShapeDtypeStruct(rope.shape, BF16),
            jax.ShapeDtypeStruct((TOK, LATENT), BF16),
            jax.ShapeDtypeStruct((LATENT, cols), F32),
            jax.ShapeDtypeStruct((LATENT, cols), F32),
        ),
        in_specs=[vmem] * 4,
        out_specs=(vmem,) * 5,
        compiler_params=pltpu.CompilerParams(vmem_limit_bytes=VMEM_LIMIT),
        name="finish",
    )(nope, rope, weight, latent)


def on_device(
    block_owner,
    query_nope,
    query_rope,
    latent_cache,
    key_up_weight,
    value_up_weight,
    saved_output,
    output_grad,
):
    return finish(
        *fused(
            block_owner,
            latent_cache,
            query_nope,
            query_rope,
            key_up_weight,
            value_up_weight,
            saved_output,
            output_grad,
        )
    )


def solution(mesh):
    return jax.shard_map(
        on_device,
        mesh=mesh,
        in_specs=(
            P("ctx"),
            P("ctx", "head"),
            P("ctx", "head"),
            P("ctx", None),
            P(None, "head"),
            P(None, "head"),
            P("ctx", "head"),
            P("ctx", "head"),
        ),
        out_specs=(
            P("ctx", "head"),
            P("ctx", "head"),
            P("ctx", None),
            P(None, "head"),
            P(None, "head"),
        ),
        check_vma=False,
    )
```

time: 930 us -> 117 us (0.13)
  waiting for transfers between devices: 704 us -> 0 us
  Pallas kernels: 0 us -> 115 us
  blocking collectives: 73.7 us -> 0 us
  matrix products: 64.6 us -> 0 us
  local copies, waits for them, and re-layouts: 30.2 us -> 1.71 us
  loops' own time: 21.4 us -> 0 us
  other arithmetic: 19.9 us -> 0 us
  between operations: 14 us -> 0.64 us
    psum x2 -> x0, waiting for transfers between devices: 445 us -> none  [the longest x1 304 us: on_device(): lax.psum(key_part.astype(jnp.bfloat16), 'ctx').astype(jnp.float32)]
    reduce_scatter x1 -> x0, waiting for transfers between devices: 223 us -> none  [on_device(): lax.psum_scatter(grad_result[1].astype(jnp.bfloat16), 'ctx', scatter_dime...]
    pallas_call x0 -> x2, Pallas kernels: none -> 115 us  [the longest x1 112 us: fused(): pl.pallas_call(fused_kernel, out_shape=(jax.ShapeDtypeStruct(query_nope.s...]
    all_gather x1 -> x0, blocking collectives: 73.7 us -> none  [on_device(): lax.all_gather(local_positions, 'ctx', axis=0, tiled=True)]
    dot_general x53 -> x0, matrix products: 64.6 us -> none  [the longest x16 29.8 us: masked_scores(): jnp.einsum('rf,kf->rk', queries, key_rows, preferred_element_type=jnp.flo...]
    all_gather x1 -> x0, waiting for transfers between devices: 35.9 us -> none  [on_device(): lax.all_gather(latent_cache, 'ctx', axis=0, tiled=True)]
    another operation x18 -> x0, loops' own time: 21.4 us -> none  [the longest x2 20.8 us: sweep_blocks(): return lax.fori_loop(0, block_turns, block_turn, carried)]
    reduce_min x16 -> x0, other arithmetic: 12 us -> none  [the longest x8 6.16 us: stat_step(): jnp.min(key_positions) <= latest_query]
  transfers between devices with their start and end apart: 4 -> 0, of which waited for: 4 -> 0; matrix products, arithmetic and copies ran while one was open for 2% -> 0% of each run, Pallas kernels for 0% -> 0%
where the time goes in v2:
time: 117 us
  Pallas kernels  115 us (98%)
  local copies, waits for them, and re-layouts  1.71 us (1%)
    pallas_call x1, Pallas kernels, fused(): pl.pallas_call(fused_kernel, out_shape=(jax.ShapeDtypeStruct(query_nope.s...  112 us
    pallas_call x1, Pallas kernels, finish(): pl.pallas_call(finish_kernel, out_shape=(jax.ShapeDtypeStruct(nope.shape,...  2.82 us

profile of v2, /device:TPU:1, one launch (start us, length us, event | category | flops | bytes accessed | tf_op | source)
XLA Modules:
  0.0 117.0 jit_solution(475527313619390116)
XLA Ops:
  0.6 1.7 %copy.13.latent = bf16[128,576]{1,0:T(8,128)(2,1)} copy(bf16[128,576]{0,1:T(8,128)(2,1)} %param.11) | data formatting | bytes 294912 | tf_op args[3]
  2.3 111.8 %fused_grads.1 = (bf16[128,512]{1,0:T(8,128)(2,1)}, bf16[128,256]{1,0:T(8,128)(2,1)}, bf16[2,2,512,256]{3,2,1,0:T(8,128)(2,1)}, bf16[2,2,4,2,16,128]{5,4,3,2,1,0:T(8,128)(2,1)}) custom-call(s32[2]{0:T(128)} %owner.1, bf16[128,576]{1,0:T(8,128)(2,1)} %copy.13.latent, bf16[128,512]{1,0:T(8,128)(2,1)} %query_nope.1, bf16[128,256]{1,0:T(8,128)(2,1)} %query_rope.1, ...), custom_call_target="tpu_custom_call" | custom-call | tf_op jit(solution)/shard_map/fused_grads/pallas_call | solution.py:636
  114.2 2.8 %finish.1 = (bf16[128,512]{1,0:T(8,128)(2,1)}, bf16[128,256]{1,0:T(8,128)(2,1)}, bf16[128,512]{1,0:T(8,128)(2,1)}, f32[512,512]{1,0:T(8,128)}, f32[512,512]{1,0:T(8,128)}) custom-call(bf16[128,512]{1,0:T(8,128)(2,1)} %get-tuple-element.9.nope, bf16[128,256]{1,0:T(8,128)(2,1)} %get-tuple-element.10.rope, bf16[2,2,512,256]{3,2,1,0:T(8,128)(2,1)} %get-tuple-element.11.weight, ...), custom_call_target="tpu_custom_call" | custom-call | tf_op jit(solution)/shard_map/finish/pallas_call | solution.py:715

commit v3 on v2

--- a/solution.py
+++ b/solution.py
@@ -67,17 +67,24 @@
 
 def fused_kernel(
     owner,
-    latent,
+    latent_t,
+    query_nope_in,
+    query_rope_in,
+    key_weight_in,
+    value_weight_in,
+    saved_in,
+    output_grad_in,
+    grad_nope,
+    grad_rope,
+    weight_all,
+    latent_out,
     query_nope,
     query_rope,
     key_weight,
     value_weight,
     saved,
     output_grad,
-    grad_nope,
-    grad_rope,
-    weight_all,
-    latent_out,
+    load_sem,
     keys,
     query_t,
     absorbed,
@@ -160,6 +167,19 @@
     def x_peer(where):
         return device(y, zh, zl, where, core)
 
+    loads = []
+    for source, dest in (
+        (query_nope_in, query_nope),
+        (key_weight_in, key_weight),
+        (query_rope_in, query_rope),
+        (value_weight_in, value_weight),
+        (output_grad_in, output_grad),
+        (saved_in, saved),
+    ):
+        loads.append(pltpu.make_async_copy(source, dest, load_sem.at[len(loads)]))
+        loads[-1].start()
+
+    latent = latent_t[...].astype(F32).T.astype(BF16)
     column = lax.broadcasted_iota(jnp.int32, (16, BLOCKS), 1)
     for side in range(2):
         mark = jnp.where(column == owner[side], 1.0, 0.0).astype(BF16)
@@ -193,6 +213,8 @@
     each(1, NZH, lambda d: near_z(d, zh).start())
     each(1, NY, lambda d: near_y(d, y).start())
 
+    for load in loads:
+        load.wait()
     rope_t = query_rope[...].astype(F32).T.astype(BF16)
     block = lax.broadcasted_iota(jnp.int32, (BLOCKS, TOK), 0)
     token = lax.broadcasted_iota(jnp.int32, (BLOCKS, TOK), 1)
@@ -426,17 +448,14 @@
         probs_low[where] = probs.astype(BF16)
         query_grad[...] += dot_tn(keys[where], grads)
 
-    each(0, chunks // 2, gradients)
-    weight_second(0)
-    each(chunks // 2, chunks, gradients)
-    weight_third(0)
-    for h in range(heads):
-        cols = slice(h * NOPE, (h + 1) * NOPE)
-        span = slice(h * TOK, (h + 1) * TOK)
-        side, at = h // (heads // 2), h % (heads // 2)
-        place = slice(at * NOPE, (at + 1) * NOPE)
-        weight_part[1, side, :, place] = dot(query_grad[:LATENT, span].astype(BF16), query_nope[:, cols]).astype(BF16)
-    weight_first(1)
+    def key_weights():
+        for h in range(heads):
+            cols = slice(h * NOPE, (h + 1) * NOPE)
+            span = slice(h * TOK, (h + 1) * TOK)
+            side, at = h // (heads // 2), h % (heads // 2)
+            place = slice(at * NOPE, (at + 1) * NOPE)
+            value = dot(query_grad[:LATENT, span].astype(BF16), query_nope[:, cols])
+            weight_part[1, side, :, place] = value.astype(BF16)
 
     wide = LATENT // NX
     size = chunks // GROUPS
@@ -505,56 +524,89 @@
 
         each(0, size, one)
 
+    def ly_copy(stage, d, src, dst):
+        return copy_to(src, dst, ly_send.at[stage, d - 1], ly_recv.at[stage, d - 1], y_peer(wrap(y + d, NY)))
+
+    def lz_copy(stage, d, src, dst):
+        return copy_to(src, dst, lz_send.at[stage, d - 1], lz_recv.at[stage, d - 1], z_peer(wrap(z + d, NZ)))
+
+    def y_first(d):
+        return ly_copy(0, d, mine.at[wrap(y + d, NY)], y_in.at[d - 1])
+
+    def z_first(d):
+        return lz_copy(0, d, mine.at[NY + wrap(z + d, NZ)], z_in.at[d - 1])
+
+    def y_second(d):
+        return ly_copy(1, d, z_sum.at[rows(wrap(y + d, NY) * 16, 16)], y_last.at[d - 1])
+
+    def z_second(d):
+        return lz_copy(1, d, y_sum.at[rows(wrap(z + d, NZ) * 16, 16)], z_last.at[d - 1])
+
+    def send_on(g):
+        def to_y(d):
+            @pl.when(wrap(y + d, NY) // size == g)
+            def _():
+                y_first(d).start()
+
+        def to_z(d):
+            @pl.when((NY + wrap(z + d, NZ)) // size == g)
+            def _():
+                z_first(d).start()
+
+        if g < GROUPS // 2:
+            each(1, NY, to_y)
+        else:
+            each(1, NZ, to_z)
+
+    def head_copy(d, who):
+        region = latent_out.at[lax.rem(who, 2), who // (2 * NX), lax.rem(who // 2, NX)]
+        return copy_to(
+            region, region, head_send.at[d - 1], head_recv.at[d - 1], (ctx, wrap(head + d, heads_all))
+        )
+
+    def grads_of(g):
+        each(g * size, (g + 1) * size, gradients)
+
+    grads_of(0)
     terms(0)
-    weight_fourth(0)
+    grads_of(1)
+    pair_sum(0)
     terms(1)
-    pair_sum(0)
-    weight_second(1)
+    weight_second(0)
+    grads_of(2)
+    pair_sum(1)
+    grads_of(3)
+    key_weights()
+    weight_first(1)
+    x_sum(0)
     terms(2)
-    pair_sum(1)
-    x_sum(0)
+    weight_third(0)
     terms(3)
     pair_sum(2)
-    weight_third(1)
     x_sum(1)
     x_last(0)
+    send_on(0)
     pair_sum(3)
-    weight_fourth(1)
     x_sum(2)
+    weight_second(1)
     x_last(1)
+    send_on(1)
+    weight_fourth(0)
     for h in range(heads):
         cols = slice(h * NOPE, (h + 1) * NOPE)
         span = slice(h * TOK, (h + 1) * TOK)
         grad_nope[:, cols] = dot_tn(query_grad[:LATENT, span].astype(BF16), key_weight[:, cols]).astype(BF16)
     x_sum(3)
     x_last(2)
+    send_on(2)
     rope_grad = jnp.concatenate(
         [query_grad[LATENT : LATENT + ROPE, h * TOK : (h + 1) * TOK] for h in range(heads)], axis=0
     )
     grad_rope[...] = rope_grad.T.astype(BF16)
     x_last(3)
-
-    def ly_copy(stage, d, src, dst):
-        return copy_to(src, dst, ly_send.at[stage, d - 1], ly_recv.at[stage, d - 1], y_peer(wrap(y + d, NY)))
-
-    def lz_copy(stage, d, src, dst):
-        return copy_to(src, dst, lz_send.at[stage, d - 1], lz_recv.at[stage, d - 1], z_peer(wrap(z + d, NZ)))
-
-    def y_first(d):
-        return ly_copy(0, d, mine.at[wrap(y + d, NY)], y_in.at[d - 1])
-
-    def z_first(d):
-        return lz_copy(0, d, mine.at[NY + wrap(z + d, NZ)], z_in.at[d - 1])
-
-    def y_second(d):
-        return ly_copy(1, d, z_sum.at[rows(wrap(y + d, NY) * 16, 16)], y_last.at[d - 1])
-
-    def z_second(d):
-        return lz_copy(1, d, y_sum.at[rows(wrap(z + d, NZ) * 16, 16)], z_last.at[d - 1])
-
-    each(1, NY, lambda d: y_first(d).start())
-    each(1, NZ, lambda d: z_first(d).start())
-    weight_last(0)
+    send_on(3)
+    weight_third(1)
+
     each(1, NY, lambda d: y_first(d).wait_recv())
     total = mine[y].astype(F32)
     for d in range(1, NY):
@@ -567,24 +619,19 @@
         total += z_in[d - 1].astype(F32)
     z_sum[...] = total.astype(BF16)
     each(1, NY, lambda d: y_second(d).start())
-
-    def head_copy(d, who):
-        region = latent_out.at[lax.rem(who, 2), who // (2 * NX), lax.rem(who // 2, NX)]
-        return copy_to(
-            region, region, head_send.at[d - 1], head_recv.at[d - 1], (ctx, wrap(head + d, heads_all))
-        )
-
     each(1, NZ, lambda d: z_second(d).wait_recv())
     total = y_sum[rows(z * 16, 16), :].astype(F32)
     for d in range(1, NZ):
         total += z_last[d - 1].astype(F32)
     latent_out[core, zl, x, 0] = total.astype(BF16)
+    weight_fourth(1)
     each(1, NY, lambda d: y_second(d).wait_recv())
     total = z_sum[rows(y * 16, 16), :].astype(F32)
     for d in range(1, NY):
         total += y_last[d - 1].astype(F32)
     latent_out[core, zl, x, 1] = total.astype(BF16)
     each(1, heads_all, lambda d: head_copy(d, head).start())
+    weight_last(0)
 
     weight_last(1)
     each(1, NZH, lambda d: near_z(d, zh).wait_send())
@@ -618,7 +665,8 @@
     each(1, heads_all, lambda d: head_copy(d, head).wait_send())
 
 
-def fused(owner, latent, query_nope, query_rope, key_weight, value_weight, saved, output_grad):
+def fused(owner, latent_t, *inputs):
+    query_nope, query_rope = inputs[:2]
     heads = query_nope.shape[1] // NOPE
     count = heads * TOK
     half = NZH * 32
@@ -641,9 +689,11 @@
             jax.ShapeDtypeStruct((2, 2, LATENT, cols), BF16),
             jax.ShapeDtypeStruct((2, 2, NX, 2, 16, wide), BF16),
         ),
-        in_specs=[pl.BlockSpec(memory_space=pltpu.SMEM)] + [vmem] * 7,
+        in_specs=[pl.BlockSpec(memory_space=pltpu.SMEM), vmem] + [pl.BlockSpec(memory_space=pl.ANY)] * 6,
         out_specs=(vmem,) * 4,
-        scratch_shapes=[
+        scratch_shapes=[hold(array.shape, BF16) for array in inputs]
+        + [
+            dma((len(inputs),)),
             hold((chunks, 2 * half, WIDE), BF16),
             hold((WIDE, count), BF16),
             hold((count, LATENT), BF16),
@@ -690,7 +740,7 @@
             collective_id=0, has_side_effects=True, vmem_limit_bytes=VMEM_LIMIT
         ),
         name="fused_grads",
-    )(owner, latent, query_nope, query_rope, key_weight, value_weight, saved, output_grad)
+    )(owner, latent_t, *inputs)
 
 
 def finish_kernel(nope, rope, weight, latent, grad_nope, grad_rope, grad_latent, grad_key, grad_value):
@@ -741,7 +791,7 @@
     return finish(
         *fused(
             block_owner,
-            latent_cache,
+            latent_cache.T,
             query_nope,
             query_rope,
             key_up_weight,

time: 117 us -> 103 us (0.88)
  Pallas kernels: 115 us -> 102 us
  local copies, waits for them, and re-layouts: 1.71 us -> 0 us
    pallas_call x1, Pallas kernels: 112 us -> 99.3 us  [fused(): pl.pallas_call(fused_kernel, out_shape=(jax.ShapeDtypeStruct(query_nope.s...]
    unnamed x1 -> x0, local copies, waits for them, and re-layouts: 1.71 us -> none
where the time goes in v3:
time: 103 us
  Pallas kernels  102 us (99%)
    pallas_call x1, Pallas kernels, fused(): pl.pallas_call(fused_kernel, out_shape=(jax.ShapeDtypeStruct(query_nope.s...  99.3 us
    pallas_call x1, Pallas kernels, finish(): pl.pallas_call(finish_kernel, out_shape=(jax.ShapeDtypeStruct(nope.shape,...  2.82 us

profile of v3, /device:TPU:1, one launch (start us, length us, event | category | flops | bytes accessed | tf_op | source)
XLA Modules:
  0.0 102.7 jit_solution(18367898760576955454)
XLA Ops:
  0.6 99.3 %fused_grads.1 = (bf16[128,512]{1,0:T(8,128)(2,1)}, bf16[128,256]{1,0:T(8,128)(2,1)}, bf16[2,2,512,256]{3,2,1,0:T(8,128)(2,1)}, bf16[2,2,4,2,16,128]{5,4,3,2,1,0:T(8,128)(2,1)}) custom-call(s32[2]{0:T(128)} %owner.1, bf16[576,128]{1,0:T(8,128)(2,1)} %bitcast.1, bf16[128,512]{1,0:T(8,128)(2,1)} %query_nope_in.1, bf16[128,256]{1,0:T(8,128)(2,1)} %query_rope_in.1, ...), custom_call_target="tpu_custom_call" | custom-call | tf_op jit(solution)/shard_map/fused_grads/pallas_call | solution.py:684
  99.9 2.8 %finish.1 = (bf16[128,512]{1,0:T(8,128)(2,1)}, bf16[128,256]{1,0:T(8,128)(2,1)}, bf16[128,512]{1,0:T(8,128)(2,1)}, f32[512,512]{1,0:T(8,128)}, f32[512,512]{1,0:T(8,128)}) custom-call(bf16[128,512]{1,0:T(8,128)(2,1)} %get-tuple-element.9.nope, bf16[128,256]{1,0:T(8,128)(2,1)} %get-tuple-element.10.rope, bf16[2,2,512,256]{3,2,1,0:T(8,128)(2,1)} %get-tuple-element.11.weight, ...), custom_call_target="tpu_custom_call" | custom-call | tf_op jit(solution)/shard_map/finish/pallas_call | solution.py:765

commit v4 on v3

--- a/solution.py
+++ b/solution.py
@@ -87,14 +87,12 @@
     load_sem,
     keys,
     query_t,
-    absorbed,
+    mixed,
     grad_out_t,
-    grad_out,
     delta,
     weights,
     prob_grad,
-    score_low,
-    probs_low,
+    low,
     tops,
     sums,
     query_grad,
@@ -279,6 +277,7 @@
         weights[where] = raised
         tops[where] = top
         sums[where] = jnp.sum(raised, axis=0, keepdims=True)
+        prob_grad[where] = raised * ((prob_grad[where] - delta[...]) * scale)
 
     each(1, NZH, lambda d: near_z(d, wrap(zh - d, NZH)).wait_recv())
     for rel in range(2):
@@ -298,12 +297,12 @@
         place = slice(at * NOPE, (at + 1) * NOPE)
         out = output_grad[:, cols]
         grads = dot_nt(out, value_weight[:, cols]).astype(BF16)
-        grad_out[span, :] = grads
+        mixed[count + h * TOK : count + (h + 1) * TOK, :] = grads
         held = saved[:, h * LATENT : (h + 1) * LATENT]
         product = grads.astype(F32) * held.astype(F32)
         delta[:, span] = jnp.sum(product.T, axis=0, keepdims=True)
         weight_part[0, side, :, place] = dot_tn(held, out).astype(BF16)
-        absorbed[span, :] = dot_nt(query_nope[:, cols], key_weight[:, cols]).astype(BF16)
+        mixed[span, :] = dot_nt(query_nope[:, cols], key_weight[:, cols]).astype(BF16)
 
     pass_copy(0, 0, y, 1 - core).wait_recv()
     pass_copy(1, 0, NY + z, 1 - core).wait_recv()
@@ -441,12 +440,16 @@
     sums[...] = shares / total[None]
     query_grad[...] = jnp.zeros_like(query_grad)
 
-    def gradients(where):
-        probs = weights[where] * sums[where]
-        grads = (probs * (prob_grad[where] - delta[...]) * scale).astype(BF16)
-        score_low[where] = grads
-        probs_low[where] = probs.astype(BF16)
-        query_grad[...] += dot_tn(keys[where], grads)
+    per_step = 4
+
+    def gradients(index):
+        span = pl.ds(index * per_step, per_step)
+        share = sums[span]
+        grads = (prob_grad[span] * share).astype(BF16)
+        low[span, :, :count] = grads
+        low[span, :, count:] = (weights[span] * share).astype(BF16)
+        flat = per_step * 2 * half
+        query_grad[...] += dot_tn(keys[span].reshape(flat, WIDE), grads.reshape(flat, count))
 
     def key_weights():
         for h in range(heads):
@@ -481,12 +484,14 @@
 
     def terms(g):
         def one(i):
-            where = g * size + i
-            value = dot(score_low[where], absorbed[...]) + dot(probs_low[where], grad_out[...])
+            span = pl.ds(g * size + i * per_step, per_step)
+            flat = per_step * 2 * half
+            block = low[span].reshape(flat, 2 * count)
+            value = (dot(block, mixed[...])).astype(BF16)
             for k in range(NX):
-                part[k, where] = value[:, k * wide : (k + 1) * wide].astype(BF16)
-
-        each(0, size, one)
+                part[k, span] = value[:, k * wide : (k + 1) * wide].reshape(per_step, 2 * half, wide)
+
+        each(0, size // per_step, one)
         pair_copy(g).start()
 
     def pair_sum(g):
@@ -565,7 +570,7 @@
         )
 
     def grads_of(g):
-        each(g * size, (g + 1) * size, gradients)
+        each(g * size // per_step, (g + 1) * size // per_step, gradients)
 
     grads_of(0)
     terms(0)
@@ -587,6 +592,16 @@
     x_last(0)
     send_on(0)
     pair_sum(3)
+    each(1, NZH, lambda d: near_z(d, zh).wait_send())
+    each(1, NY, lambda d: near_y(d, y).wait_send())
+    for axis in range(2):
+        for rel in range(2):
+            for step in range(last + 1 - rel):
+                ring_copy(axis, rel, step, ring_chunk(axis, rel, step)).wait_send()
+        pass_copy(axis, 0, y if axis == 0 else NY + z, core).wait_send()
+        for step in range(last + 1):
+            for rel in range(2 if step < last else 1):
+                pass_copy(axis, 1 + 2 * step + rel, ring_chunk(axis, rel, step + 1), core).wait_send()
     x_sum(2)
     weight_second(1)
     x_last(1)
@@ -606,6 +621,11 @@
     x_last(3)
     send_on(3)
     weight_third(1)
+    for g in range(GROUPS):
+        pair_copy(g).wait_send()
+        for kind in range(3):
+            x_copy(kind, g).wait_send()
+
 
     each(1, NY, lambda d: y_first(d).wait_recv())
     total = mine[y].astype(F32)
@@ -634,23 +654,8 @@
     weight_last(0)
 
     weight_last(1)
-    each(1, NZH, lambda d: near_z(d, zh).wait_send())
-    each(1, NY, lambda d: near_y(d, y).wait_send())
-    for axis in range(2):
-        for rel in range(2):
-            for step in range(last + 1 - rel):
-                ring_copy(axis, rel, step, ring_chunk(axis, rel, step)).wait_send()
-        pass_copy(axis, 0, y if axis == 0 else NY + z, core).wait_send()
-        for step in range(last + 1):
-            for rel in range(2 if step < last else 1):
-                pass_copy(axis, 1 + 2 * step + rel, ring_chunk(axis, rel, step + 1), core).wait_send()
     weight_sent(0)
     weight_sent(1)
-    for g in range(GROUPS):
-        pair_copy(g).wait_send()
-        for kind in range(3):
-            x_copy(kind, g).wait_send()
-
     def sent_y(d):
         y_first(d).wait_send()
         y_second(d).wait_send()
@@ -696,14 +701,12 @@
             dma((len(inputs),)),
             hold((chunks, 2 * half, WIDE), BF16),
             hold((WIDE, count), BF16),
-            hold((count, LATENT), BF16),
+            hold((2 * count, LATENT), BF16),
             hold((LATENT, count), BF16),
-            hold((count, LATENT), BF16),
             hold((1, count), F32),
             hold((chunks, 2 * half, count), F32),
             hold((chunks, 2 * half, count), F32),
-            hold((chunks, 2 * half, count), BF16),
-            hold((chunks, 2 * half, count), BF16),
+            hold((chunks, 2 * half, 2 * count), BF16),
             hold((chunks, 1, count), F32),
             hold((chunks, 1, count), F32),
             hold((WIDE, count), F32),

time: 103 us -> 101 us (0.981)
  Pallas kernels: 102 us -> 100 us
    pallas_call x1, Pallas kernels: 99.3 us -> 97.2 us  [fused(): pl.pallas_call(fused_kernel, out_shape=(jax.ShapeDtypeStruct(query_nope.s...]
where the time goes in v4:
time: 101 us
  Pallas kernels  100 us (99%)
    pallas_call x1, Pallas kernels, fused(): pl.pallas_call(fused_kernel, out_shape=(jax.ShapeDtypeStruct(query_nope.s...  97.2 us
    pallas_call x1, Pallas kernels, finish(): pl.pallas_call(finish_kernel, out_shape=(jax.ShapeDtypeStruct(nope.shape,...  2.82 us

profile of v4, /device:TPU:1, one launch (start us, length us, event | category | flops | bytes accessed | tf_op | source)
XLA Modules:
  0.0 100.6 jit_solution(17546792681043711665)
XLA Ops:
  0.6 97.2 %fused_grads.1 = (bf16[128,512]{1,0:T(8,128)(2,1)}, bf16[128,256]{1,0:T(8,128)(2,1)}, bf16[2,2,512,256]{3,2,1,0:T(8,128)(2,1)}, bf16[2,2,4,2,16,128]{5,4,3,2,1,0:T(8,128)(2,1)}) custom-call(s32[2]{0:T(128)} %owner.1, bf16[576,128]{1,0:T(8,128)(2,1)} %bitcast.1, bf16[128,512]{1,0:T(8,128)(2,1)} %query_nope_in.1, bf16[128,256]{1,0:T(8,128)(2,1)} %query_rope_in.1, ...), custom_call_target="tpu_custom_call" | custom-call | tf_op jit(solution)/shard_map/fused_grads/pallas_call | solution.py:689
  97.8 2.8 %finish.1 = (bf16[128,512]{1,0:T(8,128)(2,1)}, bf16[128,256]{1,0:T(8,128)(2,1)}, bf16[128,512]{1,0:T(8,128)(2,1)}, f32[512,512]{1,0:T(8,128)}, f32[512,512]{1,0:T(8,128)}) custom-call(bf16[128,512]{1,0:T(8,128)(2,1)} %get-tuple-element.9.nope, bf16[128,256]{1,0:T(8,128)(2,1)} %get-tuple-element.10.rope, bf16[2,2,512,256]{3,2,1,0:T(8,128)(2,1)} %get-tuple-element.11.weight, ...), custom_call_target="tpu_custom_call" | custom-call | tf_op jit(solution)/shard_map/finish/pallas_call | solution.py:768

commit v5 on v4

--- a/solution.py
+++ b/solution.py
@@ -592,6 +592,7 @@
     x_last(0)
     send_on(0)
     pair_sum(3)
+    weight_second(1)
     each(1, NZH, lambda d: near_z(d, zh).wait_send())
     each(1, NY, lambda d: near_y(d, y).wait_send())
     for axis in range(2):
@@ -603,7 +604,6 @@
             for rel in range(2 if step < last else 1):
                 pass_copy(axis, 1 + 2 * step + rel, ring_chunk(axis, rel, step + 1), core).wait_send()
     x_sum(2)
-    weight_second(1)
     x_last(1)
     send_on(1)
     weight_fourth(0)
@@ -614,13 +614,13 @@
     x_sum(3)
     x_last(2)
     send_on(2)
+    weight_third(1)
     rope_grad = jnp.concatenate(
         [query_grad[LATENT : LATENT + ROPE, h * TOK : (h + 1) * TOK] for h in range(heads)], axis=0
     )
     grad_rope[...] = rope_grad.T.astype(BF16)
     x_last(3)
     send_on(3)
-    weight_third(1)
     for g in range(GROUPS):
         pair_copy(g).wait_send()
         for kind in range(3):
@@ -639,12 +639,12 @@
         total += z_in[d - 1].astype(F32)
     z_sum[...] = total.astype(BF16)
     each(1, NY, lambda d: y_second(d).start())
+    weight_fourth(1)
     each(1, NZ, lambda d: z_second(d).wait_recv())
     total = y_sum[rows(z * 16, 16), :].astype(F32)
     for d in range(1, NZ):
         total += z_last[d - 1].astype(F32)
     latent_out[core, zl, x, 0] = total.astype(BF16)
-    weight_fourth(1)
     each(1, NY, lambda d: y_second(d).wait_recv())
     total = z_sum[rows(y * 16, 16), :].astype(F32)
     for d in range(1, NY):

time: 101 us -> 99.5 us (0.985)
  Pallas kernels: 100 us -> 98.7 us
    pallas_call x1, Pallas kernels: 97.2 us -> 95.9 us  [fused(): pl.pallas_call(fused_kernel, out_shape=(jax.ShapeDtypeStruct(query_nope.s...]
where the time goes in v5:
time: 99.5 us; the launch traced here: 99.4 us
  Pallas kernels  98.7 us (99%)
    pallas_call x1, Pallas kernels, fused(): pl.pallas_call(fused_kernel, out_shape=(jax.ShapeDtypeStruct(query_nope.s...  95.9 us
    pallas_call x1, Pallas kernels, finish(): pl.pallas_call(finish_kernel, out_shape=(jax.ShapeDtypeStruct(nope.shape,...  2.82 us

profile of v5, /device:TPU:1, one launch (start us, length us, event | category | flops | bytes accessed | tf_op | source)
XLA Modules:
  0.0 99.4 jit_solution(16100218181119211382)
XLA Ops:
  0.6 95.9 %fused_grads.1 = (bf16[128,512]{1,0:T(8,128)(2,1)}, bf16[128,256]{1,0:T(8,128)(2,1)}, bf16[2,2,512,256]{3,2,1,0:T(8,128)(2,1)}, bf16[2,2,4,2,16,128]{5,4,3,2,1,0:T(8,128)(2,1)}) custom-call(s32[2]{0:T(128)} %owner.1, bf16[576,128]{1,0:T(8,128)(2,1)} %bitcast.1, bf16[128,512]{1,0:T(8,128)(2,1)} %query_nope_in.1, bf16[128,256]{1,0:T(8,128)(2,1)} %query_rope_in.1, ...), custom_call_target="tpu_custom_call" | custom-call | tf_op jit(solution)/shard_map/fused_grads/pallas_call | solution.py:689
  96.5 2.8 %finish.1 = (bf16[128,512]{1,0:T(8,128)(2,1)}, bf16[128,256]{1,0:T(8,128)(2,1)}, bf16[128,512]{1,0:T(8,128)(2,1)}, f32[512,512]{1,0:T(8,128)}, f32[512,512]{1,0:T(8,128)}) custom-call(bf16[128,512]{1,0:T(8,128)(2,1)} %get-tuple-element.9.nope, bf16[128,256]{1,0:T(8,128)(2,1)} %get-tuple-element.10.rope, bf16[2,2,512,256]{3,2,1,0:T(8,128)(2,1)} %get-tuple-element.11.weight, ...), custom_call_target="tpu_custom_call" | custom-call | tf_op jit(solution)/shard_map/finish/pallas_call | solution.py:768

commit v6 on v5

--- a/solution.py
+++ b/solution.py
@@ -640,6 +640,10 @@
     z_sum[...] = total.astype(BF16)
     each(1, NY, lambda d: y_second(d).start())
     weight_fourth(1)
+    weight_last(0)
+    weight_sent(0)
+    each(1, NY, lambda d: y_first(d).wait_send())
+    each(1, NZ, lambda d: z_first(d).wait_send())
     each(1, NZ, lambda d: z_second(d).wait_recv())
     total = y_sum[rows(z * 16, 16), :].astype(F32)
     for d in range(1, NZ):
@@ -651,17 +655,13 @@
         total += y_last[d - 1].astype(F32)
     latent_out[core, zl, x, 1] = total.astype(BF16)
     each(1, heads_all, lambda d: head_copy(d, head).start())
-    weight_last(0)
 
     weight_last(1)
-    weight_sent(0)
     weight_sent(1)
     def sent_y(d):
-        y_first(d).wait_send()
         y_second(d).wait_send()
 
     def sent_z(d):
-        z_first(d).wait_send()
         z_second(d).wait_send()
 
     each(1, NY, sent_y)

time: 99.5 us -> 99.5 us (level)
  no operation moved by 1% of the time
where the time goes in v6:
time: 99.5 us; the launch traced here: 99.4 us
  Pallas kernels  98.7 us (99%)
    pallas_call x1, Pallas kernels, fused(): pl.pallas_call(fused_kernel, out_shape=(jax.ShapeDtypeStruct(query_nope.s...  95.9 us
    pallas_call x1, Pallas kernels, finish(): pl.pallas_call(finish_kernel, out_shape=(jax.ShapeDtypeStruct(nope.shape,...  2.82 us

profile of v6, /device:TPU:1, one launch (start us, length us, event | category | flops | bytes accessed | tf_op | source)
XLA Modules:
  0.0 99.4 jit_solution(9465562542466933184)
XLA Ops:
  0.6 95.9 %fused_grads.1 = (bf16[128,512]{1,0:T(8,128)(2,1)}, bf16[128,256]{1,0:T(8,128)(2,1)}, bf16[2,2,512,256]{3,2,1,0:T(8,128)(2,1)}, bf16[2,2,4,2,16,128]{5,4,3,2,1,0:T(8,128)(2,1)}) custom-call(s32[2]{0:T(128)} %owner.1, bf16[576,128]{1,0:T(8,128)(2,1)} %bitcast.1, bf16[128,512]{1,0:T(8,128)(2,1)} %query_nope_in.1, bf16[128,256]{1,0:T(8,128)(2,1)} %query_rope_in.1, ...), custom_call_target="tpu_custom_call" | custom-call | tf_op jit(solution)/shard_map/fused_grads/pallas_call | solution.py:689
  96.5 2.8 %finish.1 = (bf16[128,512]{1,0:T(8,128)(2,1)}, bf16[128,256]{1,0:T(8,128)(2,1)}, bf16[128,512]{1,0:T(8,128)(2,1)}, f32[512,512]{1,0:T(8,128)}, f32[512,512]{1,0:T(8,128)}) custom-call(bf16[128,512]{1,0:T(8,128)(2,1)} %get-tuple-element.9.nope, bf16[128,256]{1,0:T(8,128)(2,1)} %get-tuple-element.10.rope, bf16[2,2,512,256]{3,2,1,0:T(8,128)(2,1)} %get-tuple-element.11.weight, ...), custom_call_target="tpu_custom_call" | custom-call | tf_op jit(solution)/shard_map/finish/pallas_call | solution.py:768
